TPU v7x, 128 devices: a whole 4x4x4 slice. The times are simulated.
128 devices in a mesh: sub: 8 (over x_hi, z), stn: 16 (over y, x_lo, core).
Axes of the slice: x: 4 (x_hi: 2, x_lo: 2; x = x_hi * 2 + x_lo), y: 4, z: 4, core: 2. Of those that a mesh axis runs over, the one named last changes fastest.
Arguments:
- samples: bfloat16 [512, 524288], P('stn', 'sub'), may hold values from -8 to 7, as said below
- taps: int32 [4096], replicated, may hold values from -64 to 64
Outputs:
- visibility: bfloat16 [16, 512, 288, 128], P('sub', 'stn')
Inputs may be any that keep to these rules, and one draw needn't show every extreme that they name: `samples`: whole numbers.
All inputs are finite; a program needn't handle non-finite values.
Results may differ from a plain program's by a relative error of at most 0.0073.
Values may be sent and summed in bfloat16 or wider, within the bound.
No kernel may reach another device: no remote copies, remote signals or barrier semaphores. Data moves between devices by JAX's collectives and lax.ppermute only.
A program may use at most 128 MiB of HBM per device.

v0:
```python
import math

import jax
import jax.numpy as jnp
from jax import lax
from jax.sharding import PartitionSpec as P

BRANCHES = 256
TAPS = 16
LAGS = 128
SUB_DEV = 2
T_DEV = 256


def shifted_2(value, axis, steps):
    count = lax.axis_size(axis)
    first, last = (max(0, -steps), min(count, count - steps))
    return lax.ppermute(value, axis, [(source, source + steps) for source in range(first, last)])


def passed_along(value, axis, steps):
    count = lax.axis_size(axis)
    pairs = [(source, (source + steps) % count) for source in range(count)]
    return lax.ppermute(value, axis, pairs)


def cosine_matrix(count, branches):
    band = (branches // 2 - count // 2 + jnp.arange(count, dtype=jnp.int32)).astype(
        jnp.float32
    ) + 0.5
    filter_arm = jnp.arange(branches, dtype=jnp.int32).astype(jnp.float32) + 0.5
    values = jnp.cos(math.pi / branches * band[:, None] * filter_arm[None, :]) * (
        math.sqrt(2.0 / branches) / 512.0
    )
    return values.astype(jnp.bfloat16)


def lag_products(toeplitz_matrix, partner, half, scale):
    width = toeplitz_matrix.shape[-1]
    rows = partner.shape[1]
    padded = jnp.pad(partner, ((0, 0), (0, 0), (half, half)))
    stacked_frames = jnp.concatenate([padded[:, :, :width], padded[:, :, half:]], axis=1)
    paired_result = jnp.einsum(
        "jmpv,jzv->jmzp", toeplitz_matrix, stacked_frames, preferred_element_type=jnp.float32
    )
    joined = jnp.concatenate([paired_result[:, :, :rows], paired_result[:, :, rows:]], axis=-1)
    return (joined * scale).astype(jnp.bfloat16)


def body(samples, taps):
    block = samples.shape[0]
    memory_length = (TAPS - 1) * BRANCHES
    tap_table = taps.reshape(TAPS, BRANCHES).astype(jnp.float32)
    owners = lax.axis_size("sub")
    table = cosine_matrix(SUB_DEV * owners, BRANCHES)
    tail = samples[:, samples.shape[1] - memory_length :]
    earlier = shifted_2(tail, "sub", 1)
    frames = (
        jnp.concatenate([earlier, samples], axis=1).astype(jnp.float32).reshape(block, -1, BRANCHES)
    )
    filtered = tap_table[0] * frames[:, 0:T_DEV]
    for branch_step in range(1, TAPS):
        filtered = filtered + tap_table[branch_step] * frames[:, branch_step : branch_step + T_DEV]
    modulate_filtered = filtered.astype(jnp.bfloat16)
    count = modulate_filtered.shape[1]
    flat = modulate_filtered.reshape(block * count, BRANCHES)
    spectra = lax.dot_general(
        table, flat, (((1,), (1,)), ((), ())), preferred_element_type=jnp.float32
    )
    spectra = spectra.reshape(-1, block, count)
    bands = spectra.astype(jnp.bfloat16)
    own = lax.all_to_all(bands, "sub", split_axis=0, concat_axis=2, tiled=True)
    band_count = own.shape[0]
    total_time = own.shape[2]
    half = LAGS // 2
    scale = 1.0 / math.sqrt(T_DEV * owners)
    padded_own = jnp.pad(own, ((0, 0), (0, 0), (half, half)))
    shifted = padded_own[:, :, 1:]
    span = shifted.shape[2]
    tiled = jnp.tile(shifted, (1, 1, half + 1))
    skewed = tiled[:, :, : half * (span + 1)].reshape(band_count, block, half, span + 1)
    toeplitz_matrix = jnp.flip(skewed[:, :, :, : total_time + half], axis=2)
    cycle_size = lax.axis_size("stn")
    reach = cycle_size // 2
    slots = [lag_products(toeplitz_matrix, own, half, scale)] + [None] * reach
    held = own
    for step in range(1, reach + 1):
        held = passed_along(held, "stn", -1)
        slots[step] = lag_products(toeplitz_matrix, held, half, scale)
    return jnp.concatenate(slots, axis=2)


def solution(mesh):
    in_specs = (P("stn", "sub"), P())
    out_specs = P("sub", "stn", None, None)
    return jax.shard_map(body, mesh=mesh, in_specs=in_specs, out_specs=out_specs, check_vma=False)
```

profile of v0, /device:TPU:27, one launch (start us, length us, event | category | flops | bytes accessed | tf_op | source)
XLA Modules:
  0.0 355.0 jit_solution(5692862149219543510)
XLA Ops:
  0.0 1.0 slice.233
  1.0 3.6 %collective-permute-start = (bf16[32,3840]{1,0:T(8,128)(2,1)S(1)}, bf16[32,3840]{1,0:T(8,128)(2,1)S(1)}, u32[]{:S(2)}, u32[]{:S(2)}) collective-permute-start(bf16[32,3840]{1,0:T(8,128)(2,1)S(1)} %slice.233), channel_id=1, source_target_pairs={{0,16},{16,32},{32,48},{48,64},{64,80},{80,96},{96,112},{1,17},{17... | collective-permute-start | bytes 737288 | tf_op jit(solution)/shard_map/ppermute | solution.py:18
  4.5 0.7 convert_element_type.75
  5.3 3.8 %collective-permute-done = bf16[32,3840]{1,0:T(8,128)(2,1)S(1)} collective-permute-done((bf16[32,3840]{1,0:T(8,128)(2,1)S(1)}, bf16[32,3840]{1,0:T(8,128)(2,1)S(1)}, u32[]{:S(2)}, u32[]{:S(2)}) %collective-permute-start) | collective-permute-done | bytes 245792 | tf_op jit(solution)/shard_map/ppermute | solution.py:18
  9.1 6.2 %maximum_convert_fusion = f32[32,69376]{1,0:T(8,128)} fusion(bf16[32,65536]{1,0:T(8,128)(2,1)} %param.2, bf16[32,3840]{1,0:T(8,128)(2,1)S(1)} %collective-permute-done), kind=kLoop, calls=%fused_computation.32 | loop fusion | flops 8880128 | bytes 13320192 | tf_op jit(solution)/shard_map/convert_element_type | solution.py:59
  15.4 7.7 %reshape.79 = f32[32,271,256]{2,1,0:T(8,128)} reshape(f32[32,69376]{1,0:T(8,128)} %maximum_convert_fusion) | data formatting | bytes 17760256 | tf_op jit(solution)/shard_map/convert_element_type | solution.py:59
  23.1 54.4 %fusion.18 = bf16[16,32,256]{2,0,1:T(8,128)(2,1)S(1)} fusion(f32[32,271,256]{2,1,0:T(8,128)} %reshape.79, f32[256]{0:T(256)S(1)} %get-tuple-element.42, f32[256]{0:T(256)S(1)} %get-tuple-element.43, f32[256]{0:T(256)S(1)} %get-tuple-element.44, f32[256]{0:T(256)S(1)} %get-tuple-element.45, f32[256]{0:T(256)S(1)} %get-tuple-element.46, ...), kind=kOutput, calls=%fused_computation.43 | convolution fusion | flops 134361088 | bytes 134497344 | tf_op jit(solution)/shard_map/dot_general | solution.py:67
  77.6 14.7 %all_to_all.18 = bf16[16,32,256]{2,1,0:T(8,128)(2,1)S(1)} all-to-all(bf16[16,32,256]{2,1,0:T(8,128)(2,1)S(1)} %copy.5), channel_id=1, replica_groups=mesh['sub'=8,'stn'=16] {'sub'}, dimensions={0} | all-to-all | bytes 524288 | tf_op jit(solution)/shard_map/all_to_all | solution.py:72
  92.7 3.5 collective-permute-start.1
  96.3 8.3 %tile.4 = bf16[2,32,65,2175]{3,2,1,0:T(8,128)(2,1)} broadcast(bf16[2,32,2175]{2,1,0:T(8,128)(2,1)S(1)} %pad_slice_fusion.16), dimensions={0,1,3} | broadcast | bytes 18374400 | tf_op jit(solution)/shard_map/tile | solution.py:80
  104.6 20.2 %tile.10 = bf16[2,32,141375]{2,1,0:T(8,128)(2,1)} reshape(bf16[2,32,65,2175]{3,2,1,0:T(8,128)(2,1)} %tile.4) | data formatting | bytes 36192000 | tf_op jit(solution)/shard_map/tile | solution.py:80
  124.8 6.1 %slice-done = bf16[2,32,139264]{2,1,0:T(8,128)(2,1)S(1)} async-done(((bf16[2,32,141375]{2,1,0:T(8,128)(2,1)}), bf16[2,32,139264]{2,1,0:T(8,128)(2,1)S(1)}, s32[]{:S(2)}) %slice-start) | async-done | bytes 17825816 | tf_op jit(solution)/shard_map/slice | solution.py:81
  130.9 7.7 %copy.16 = bf16[8,8,64,2176]{3,2,1,0:T(8,128)(2,1)} copy(bf16[8,8,64,2176]{3,1,2,0:T(8,128)(2,1)S(1)} %bitcast.86) | data formatting | bytes 35651584
  138.6 42.1 %rev.4 = bf16[2,32,64,2112]{3,2,1,0:T(8,128)(2,1)} reverse(bf16[2,32,64,2112]{3,2,1,0:T(8,128)(2,1)} %bitcast.87), dimensions={2} | reverse | bytes 34603008 | tf_op jit(solution)/shard_map/jit(_flip)/rev | solution.py:82
  180.7 12.7 %convolution_bitcast_fusion.8 = f32[2,32,64,64]{3,2,1,0:T(8,128)S(1)} fusion(bf16[2,32,64,2112]{3,2,1,0:T(8,128)(2,1)} %rev.4, bf16[2,32,2112]{2,1,0:T(8,128)(2,1)S(1)} %get-tuple-element.40, bf16[2,32,2112]{2,1,0:T(8,128)(2,1)S(1)} %get-tuple-element.39), kind=kOutput, calls=%fused_computation.42 | convolution fusion | flops 1108377600 | bytes 18890752 | tf_op jit(solution)/shard_map/jmpv,jzv->jmzp/dot_general | solution.py:43
  193.3 0.2 fusion.80
  193.5 1.1 fusion.56
  194.8 12.7 %convolution_bitcast_fusion.7 = f32[2,32,64,64]{3,2,1,0:T(8,128)S(1)} fusion(bf16[2,32,64,2112]{3,2,1,0:T(8,128)(2,1)} %rev.4, bf16[2,32,2112]{2,1,0:T(8,128)(2,1)S(1)} %get-tuple-element.38, bf16[2,32,2112]{2,1,0:T(8,128)(2,1)S(1)} %get-tuple-element.37), kind=kOutput, calls=%fused_computation.41 | convolution fusion | flops 1108377600 | bytes 18890752 | tf_op jit(solution)/shard_map/jmpv,jzv->jmzp/dot_general | solution.py:43
  207.8 1.1 fusion.55
  208.9 6.5 %collective-permute-done.2 = bf16[2,32,2048]{2,1,0:T(8,128)(2,1)S(1)} collective-permute-done((bf16[2,32,2048]{2,1,0:T(8,128)(2,1)S(1)}, bf16[2,32,2048]{2,1,0:T(8,128)(2,1)S(1)}, u32[]{:S(2)}, u32[]{:S(2)}) %collective-permute-start.2) | collective-permute-done | bytes 262176 | tf_op jit(solution)/shard_map/ppermute | solution.py:24
  215.6 12.7 %convolution_bitcast_fusion.6 = f32[2,32,64,64]{3,2,1,0:T(8,128)S(1)} fusion(bf16[2,32,64,2112]{3,2,1,0:T(8,128)(2,1)} %rev.4, bf16[2,32,2112]{2,1,0:T(8,128)(2,1)S(1)} %get-tuple-element.36, bf16[2,32,2112]{2,1,0:T(8,128)(2,1)S(1)} %get-tuple-element.35), kind=kOutput, calls=%fused_computation.40 | convolution fusion | flops 1108377600 | bytes 18890752 | tf_op jit(solution)/shard_map/jmpv,jzv->jmzp/dot_general | solution.py:43
  228.3 0.2 collective-permute-start.3
  228.5 0.2 fusion.78
  228.7 1.1 fusion.54
  229.9 6.5 %collective-permute-done.3 = bf16[2,32,2048]{2,1,0:T(8,128)(2,1)S(1)} collective-permute-done((bf16[2,32,2048]{2,1,0:T(8,128)(2,1)S(1)}, bf16[2,32,2048]{2,1,0:T(8,128)(2,1)S(1)}, u32[]{:S(2)}, u32[]{:S(2)}) %collective-permute-start.3) | collective-permute-done | bytes 262176 | tf_op jit(solution)/shard_map/ppermute | solution.py:24
  236.6 12.7 %convolution_bitcast_fusion.5 = f32[2,32,64,64]{3,2,1,0:T(8,128)S(1)} fusion(bf16[2,32,64,2112]{3,2,1,0:T(8,128)(2,1)} %rev.4, bf16[2,32,2112]{2,1,0:T(8,128)(2,1)S(1)} %get-tuple-element.34, bf16[2,32,2112]{2,1,0:T(8,128)(2,1)S(1)} %get-tuple-element.33), kind=kOutput, calls=%fused_computation.39 | convolution fusion | flops 1108377600 | bytes 18890752 | tf_op jit(solution)/shard_map/jmpv,jzv->jmzp/dot_general | solution.py:43
  249.3 0.2 fusion.77
  249.5 1.1 fusion.53
  250.7 6.5 %collective-permute-done.4 = bf16[2,32,2048]{2,1,0:T(8,128)(2,1)S(1)} collective-permute-done((bf16[2,32,2048]{2,1,0:T(8,128)(2,1)S(1)}, bf16[2,32,2048]{2,1,0:T(8,128)(2,1)S(1)}, u32[]{:S(2)}, u32[]{:S(2)}) %collective-permute-start.4) | collective-permute-done | bytes 262176 | tf_op jit(solution)/shard_map/ppermute | solution.py:24
  257.4 12.7 %convolution_bitcast_fusion.4 = f32[2,32,64,64]{3,2,1,0:T(8,128)S(1)} fusion(bf16[2,32,64,2112]{3,2,1,0:T(8,128)(2,1)} %rev.4, bf16[2,32,2112]{2,1,0:T(8,128)(2,1)S(1)} %get-tuple-element.32, bf16[2,32,2112]{2,1,0:T(8,128)(2,1)S(1)} %get-tuple-element.31), kind=kOutput, calls=%fused_computation.38 | convolution fusion | flops 1108377600 | bytes 18890752 | tf_op jit(solution)/shard_map/jmpv,jzv->jmzp/dot_general | solution.py:43
  270.1 0.2 fusion.76
  270.3 1.1 fusion.52
  271.5 6.5 %collective-permute-done.5 = bf16[2,32,2048]{2,1,0:T(8,128)(2,1)S(1)} collective-permute-done((bf16[2,32,2048]{2,1,0:T(8,128)(2,1)S(1)}, bf16[2,32,2048]{2,1,0:T(8,128)(2,1)S(1)}, u32[]{:S(2)}, u32[]{:S(2)}) %collective-permute-start.5) | collective-permute-done | bytes 262176 | tf_op jit(solution)/shard_map/ppermute | solution.py:24
  278.2 12.7 %convolution_bitcast_fusion.3 = f32[2,32,64,64]{3,2,1,0:T(8,128)S(1)} fusion(bf16[2,32,64,2112]{3,2,1,0:T(8,128)(2,1)} %rev.4, bf16[2,32,2112]{2,1,0:T(8,128)(2,1)S(1)} %get-tuple-element.30, bf16[2,32,2112]{2,1,0:T(8,128)(2,1)S(1)} %get-tuple-element.29), kind=kOutput, calls=%fused_computation.37 | convolution fusion | flops 1108377600 | bytes 18890752 | tf_op jit(solution)/shard_map/jmpv,jzv->jmzp/dot_general | solution.py:43
  290.9 0.3 collective-permute-start.6
  291.2 0.2 fusion.75
  291.4 1.1 fusion.51
  292.5 6.5 %collective-permute-done.6 = bf16[2,32,2048]{2,1,0:T(8,128)(2,1)S(1)} collective-permute-done((bf16[2,32,2048]{2,1,0:T(8,128)(2,1)S(1)}, bf16[2,32,2048]{2,1,0:T(8,128)(2,1)S(1)}, u32[]{:S(2)}, u32[]{:S(2)}) %collective-permute-start.6) | collective-permute-done | bytes 262176 | tf_op jit(solution)/shard_map/ppermute | solution.py:24
  299.2 12.7 %convolution_bitcast_fusion.2 = f32[2,32,64,64]{3,2,1,0:T(8,128)S(1)} fusion(bf16[2,32,64,2112]{3,2,1,0:T(8,128)(2,1)} %rev.4, bf16[2,32,2112]{2,1,0:T(8,128)(2,1)S(1)} %get-tuple-element.28, bf16[2,32,2112]{2,1,0:T(8,128)(2,1)S(1)} %get-tuple-element.27), kind=kOutput, calls=%fused_computation.36 | convolution fusion | flops 1108377600 | bytes 18890752 | tf_op jit(solution)/shard_map/jmpv,jzv->jmzp/dot_general | solution.py:43
  311.9 0.2 fusion.74
  312.2 1.1 fusion.50
  313.3 6.5 %collective-permute-done.7 = bf16[2,32,2048]{2,1,0:T(8,128)(2,1)S(1)} collective-permute-done((bf16[2,32,2048]{2,1,0:T(8,128)(2,1)S(1)}, bf16[2,32,2048]{2,1,0:T(8,128)(2,1)S(1)}, u32[]{:S(2)}, u32[]{:S(2)}) %collective-permute-start.7) | collective-permute-done | bytes 262176 | tf_op jit(solution)/shard_map/ppermute | solution.py:24
  320.0 12.7 %convolution_bitcast_fusion.1 = f32[2,32,64,64]{3,2,1,0:T(8,128)S(1)} fusion(bf16[2,32,64,2112]{3,2,1,0:T(8,128)(2,1)} %rev.4, bf16[2,32,2112]{2,1,0:T(8,128)(2,1)S(1)} %get-tuple-element.26, bf16[2,32,2112]{2,1,0:T(8,128)(2,1)S(1)} %get-tuple-element.25), kind=kOutput, calls=%fused_computation.35 | convolution fusion | flops 1108377600 | bytes 18890752 | tf_op jit(solution)/shard_map/jmpv,jzv->jmzp/dot_general | solution.py:43
  332.7 0.2 fusion.73
  333.0 1.1 fusion.49
  334.1 6.5 %collective-permute-done.8 = bf16[2,32,2048]{2,1,0:T(8,128)(2,1)S(1)} collective-permute-done((bf16[2,32,2048]{2,1,0:T(8,128)(2,1)S(1)}, bf16[2,32,2048]{2,1,0:T(8,128)(2,1)S(1)}, u32[]{:S(2)}, u32[]{:S(2)}) %collective-permute-start.8) | collective-permute-done | bytes 262176 | tf_op jit(solution)/shard_map/ppermute | solution.py:24
  340.8 12.7 %convolution_bitcast_fusion = f32[2,32,64,64]{3,2,1,0:T(8,128)S(1)} fusion(bf16[2,32,64,2112]{3,2,1,0:T(8,128)(2,1)} %rev.4, bf16[2,32,2112]{2,1,0:T(8,128)(2,1)S(1)} %get-tuple-element.24, bf16[2,32,2112]{2,1,0:T(8,128)(2,1)S(1)} %get-tuple-element.23), kind=kOutput, calls=%fused_computation.34 | convolution fusion | flops 1108377600 | bytes 18890752 | tf_op jit(solution)/shard_map/jmpv,jzv->jmzp/dot_general | solution.py:43
  353.7 1.1 fusion.48
  (24 shorter events, 2.6 us)
Async XLA Ops:
  1.0 8.2 %collective-permute-start = (bf16[32,3840]{1,0:T(8,128)(2,1)S(1)}, bf16[32,3840]{1,0:T(8,128)(2,1)S(1)}, u32[]{:S(2)}, u32[]{:S(2)}) collective-permute-start(bf16[32,3840]{1,0:T(8,128)(2,1)S(1)} %slice.233), channel_id=1, source_target_pairs={{0,16},{16,32},{32,48},{48,64},{64,80},{80,96},{96,112},{1,17},{17... | collective-permute-start | bytes 737288 | tf_op jit(solution)/shard_map/ppermute | solution.py:18
  92.7 101.9 %collective-permute-start.1 = (bf16[2,32,2048]{2,1,0:T(8,128)(2,1)S(1)}, bf16[2,32,2048]{2,1,0:T(8,128)(2,1)S(1)}, u32[]{:S(2)}, u32[]{:S(2)}) collective-permute-start(bf16[2,32,2048]{2,1,0:T(8,128)(2,1)S(1)} %all_to_all.16), channel_id=1, source_target_pairs={{0,15},{1,0},{2,1},{3,2},{4,3},{5,4},{6,5},{7,6},{8,7},{9,8},{10,9... | collective-permute-start | bytes 786440 | tf_op jit(solution)/shard_map/ppermute | solution.py:24
  124.8 6.1 %slice-start = ((bf16[2,32,141375]{2,1,0:T(8,128)(2,1)}), bf16[2,32,139264]{2,1,0:T(8,128)(2,1)S(1)}, s32[]{:S(2)}) async-start(bf16[2,32,141375]{2,1,0:T(8,128)(2,1)} %tile.10), calls=%async_computation.1 | async-start | bytes 35651584 | tf_op jit(solution)/shard_map/slice | solution.py:81
  207.5 8.0 %collective-permute-start.2 = (bf16[2,32,2048]{2,1,0:T(8,128)(2,1)S(1)}, bf16[2,32,2048]{2,1,0:T(8,128)(2,1)S(1)}, u32[]{:S(2)}, u32[]{:S(2)}) collective-permute-start(bf16[2,32,2048]{2,1,0:T(8,128)(2,1)S(1)} %collective-permute-done.1), channel_id=1, source_target_pairs={{0,15},{1,0},{2,1},{3,2},{4,3},{5,4},{6,5},{7,6},{8,7},{9,8},{10,9... | collective-permute-start | bytes 786440 | tf_op jit(solution)/shard_map/ppermute | solution.py:24
  228.3 8.1 %collective-permute-start.3 = (bf16[2,32,2048]{2,1,0:T(8,128)(2,1)S(1)}, bf16[2,32,2048]{2,1,0:T(8,128)(2,1)S(1)}, u32[]{:S(2)}, u32[]{:S(2)}) collective-permute-start(bf16[2,32,2048]{2,1,0:T(8,128)(2,1)S(1)} %collective-permute-done.2), channel_id=1, source_target_pairs={{0,15},{1,0},{2,1},{3,2},{4,3},{5,4},{6,5},{7,6},{8,7},{9,8},{10,9... | collective-permute-start | bytes 786440 | tf_op jit(solution)/shard_map/ppermute | solution.py:24
  249.3 8.0 %collective-permute-start.4 = (bf16[2,32,2048]{2,1,0:T(8,128)(2,1)S(1)}, bf16[2,32,2048]{2,1,0:T(8,128)(2,1)S(1)}, u32[]{:S(2)}, u32[]{:S(2)}) collective-permute-start(bf16[2,32,2048]{2,1,0:T(8,128)(2,1)S(1)} %collective-permute-done.3), channel_id=1, source_target_pairs={{0,15},{1,0},{2,1},{3,2},{4,3},{5,4},{6,5},{7,6},{8,7},{9,8},{10,9... | collective-permute-start | bytes 786440 | tf_op jit(solution)/shard_map/ppermute | solution.py:24
  270.1 8.0 %collective-permute-start.5 = (bf16[2,32,2048]{2,1,0:T(8,128)(2,1)S(1)}, bf16[2,32,2048]{2,1,0:T(8,128)(2,1)S(1)}, u32[]{:S(2)}, u32[]{:S(2)}) collective-permute-start(bf16[2,32,2048]{2,1,0:T(8,128)(2,1)S(1)} %collective-permute-done.4), channel_id=1, source_target_pairs={{0,15},{1,0},{2,1},{3,2},{4,3},{5,4},{6,5},{7,6},{8,7},{9,8},{10,9... | collective-permute-start | bytes 786440 | tf_op jit(solution)/shard_map/ppermute | solution.py:24
  290.9 8.2 %collective-permute-start.6 = (bf16[2,32,2048]{2,1,0:T(8,128)(2,1)S(1)}, bf16[2,32,2048]{2,1,0:T(8,128)(2,1)S(1)}, u32[]{:S(2)}, u32[]{:S(2)}) collective-permute-start(bf16[2,32,2048]{2,1,0:T(8,128)(2,1)S(1)} %collective-permute-done.5), channel_id=1, source_target_pairs={{0,15},{1,0},{2,1},{3,2},{4,3},{5,4},{6,5},{7,6},{8,7},{9,8},{10,9... | collective-permute-start | bytes 786440 | tf_op jit(solution)/shard_map/ppermute | solution.py:24
  311.9 8.0 %collective-permute-start.7 = (bf16[2,32,2048]{2,1,0:T(8,128)(2,1)S(1)}, bf16[2,32,2048]{2,1,0:T(8,128)(2,1)S(1)}, u32[]{:S(2)}, u32[]{:S(2)}) collective-permute-start(bf16[2,32,2048]{2,1,0:T(8,128)(2,1)S(1)} %collective-permute-done.6), channel_id=1, source_target_pairs={{0,15},{1,0},{2,1},{3,2},{4,3},{5,4},{6,5},{7,6},{8,7},{9,8},{10,9... | collective-permute-start | bytes 786440 | tf_op jit(solution)/shard_map/ppermute | solution.py:24
  332.7 8.0 %collective-permute-start.8 = (bf16[2,32,2048]{2,1,0:T(8,128)(2,1)S(1)}, bf16[2,32,2048]{2,1,0:T(8,128)(2,1)S(1)}, u32[]{:S(2)}, u32[]{:S(2)}) collective-permute-start(bf16[2,32,2048]{2,1,0:T(8,128)(2,1)S(1)} %collective-permute-done.7), channel_id=1, source_target_pairs={{0,15},{1,0},{2,1},{3,2},{4,3},{5,4},{6,5},{7,6},{8,7},{9,8},{10,9... | collective-permute-start | bytes 786440 | tf_op jit(solution)/shard_map/ppermute | solution.py:24
where the time goes:
time: 361 us; the launch traced here: 355 us
  matrix products  168 us (47%)
  local copies, waits for them, and re-layouts  96.5 us (27%)
  waiting for transfers between devices  49.7 us (14%)
  other arithmetic  17.3 us (5%)
  blocking collectives  14.7 us (4%)
  starting transfers between devices  7.94 us (2%)
    dot_general x9, matrix products, lag_products(): jnp.einsum('jmpv,jzv->jmzp', toeplitz_matrix, stacked_frames, preferred_e...  114 us
    dot_general x1, matrix products, body(): lax.dot_general(table, flat, (((1,), (1,)), ((), ())), preferred_element_...  54.4 us
    ppermute x8, waiting for transfers between devices, passed_along(): return lax.ppermute(value, axis, pairs)  45.8 us
    rev x1, local copies, waits for them, and re-layouts, body(): toeplitz_matrix = jnp.flip(skewed[:, :, :, :total_time + half], axis=2)  42.1 us
    another operation x2, local copies, waits for them, and re-layouts, body(): tiled = jnp.tile(shifted, (1, 1, half + 1))  28.5 us
    all_to_all x1, blocking collectives, body(): own = lax.all_to_all(bands, 'sub', split_axis=0, concat_axis=2, tiled=True)  14.7 us
    unnamed x8, other arithmetic  9.13 us
    convert_element_type x1, local copies, waits for them, and re-layouts, body(): jnp.concatenate([earlier, samples], axis=1).astype(jnp.float32)  7.72 us
  transfers between devices with their start and end apart: 9, of which 8 were waited for; matrix products, arithmetic and copies ran while one was open for 29% of the time, Pallas kernels for 0%

commit v1 on v0

v1 whole, which is shorter than its diff:
```python
import functools
import math

import jax
import jax.numpy as jnp
import numpy as np
from jax import lax
from jax.experimental import pallas as pl
from jax.experimental.pallas import tpu as pltpu
from jax.sharding import Mesh
from jax.sharding import PartitionSpec as P

BRANCHES = 256
TAPS = 16
LAGS = 128
T_DEV = 256
SUBBANDS = 16
BLOCK = 32
N_SUB = 8
CHIPS = 8
TOTAL = T_DEV * N_SUB
TAIL = 128
CHUNK = 32
REACH = 4
LANE = 128


def cosine_matrix():
    band = np.float32(BRANCHES // 2 - SUBBANDS // 2) + np.arange(SUBBANDS, dtype=np.float32)
    band = band + np.float32(0.5)
    arm = np.arange(BRANCHES, dtype=np.float32) + np.float32(0.5)
    angle = np.float32(math.pi / BRANCHES) * band[:, None] * arm[None, :]
    table = np.cos(angle) * np.float32(math.sqrt(2.0 / BRANCHES) / 512.0)
    return jnp.asarray(table).astype(jnp.bfloat16).astype(jnp.float32)


def nt_dot(a, b):
    return lax.dot_general(a, b, (((1,), (1,)), ((), ())), preferred_element_type=jnp.float32)


def shift_lanes(tiles, steps, lane, grow):
    rolled = [pltpu.roll(t, steps, 1) for t in tiles]
    outside = jnp.zeros_like(rolled[0])
    result = [jnp.where(lane < steps, outside, rolled[0])]
    for before, after in zip(rolled[:-1], rolled[1:]):
        result.append(jnp.where(lane < steps, before, after))
    if grow:
        result.append(jnp.where(lane < steps, rolled[-1], outside))
    return result


def filter_kernel(x_ref, taps_ref, cos_ref, out_ref, frames_ref, weight_ref, bands_ref):
    step = pl.program_id(0)
    for frame in range(CHUNK):
        row = pl.multiple_of((step * CHUNK + frame) * BLOCK, BLOCK)
        for half in range(2):
            start = frame * BRANCHES + half * LANE
            frames_ref[half, pl.ds(row, BLOCK), :] = x_ref[:, start : start + LANE].astype(
                jnp.float32
            )

    @pl.when(step == pl.num_programs(0) - 1)
    def _():
        table = cos_ref[...]
        for tap in range(TAPS):
            product = table * taps_ref[tap : tap + 1, :].astype(jnp.float32)
            high = product.astype(jnp.bfloat16)
            low = (product - high.astype(jnp.float32)).astype(jnp.bfloat16)
            weight_ref[0, tap * SUBBANDS : (tap + 1) * SUBBANDS, :] = high
            weight_ref[1, tap * SUBBANDS : (tap + 1) * SUBBANDS, :] = low

        lane = lax.broadcasted_iota(jnp.int32, (SUBBANDS, LANE), 1)

        def one_input(i, carry):
            data = jnp.concatenate(
                [frames_ref[half, pl.ds(i, T_DEV, stride=BLOCK), :] for half in range(2)], axis=1
            ).astype(jnp.bfloat16)
            products = nt_dot(weight_ref[0], data) + nt_dot(weight_ref[1], data)
            level = []
            for tap in range(TAPS):
                part = products[tap * SUBBANDS : (tap + 1) * SUBBANDS]
                level.append([part[:, :LANE], part[:, LANE:]])
            steps = 1
            while len(level) > 1:
                merged = []
                for first, second in zip(level[0::2], level[1::2]):
                    moved = shift_lanes(first, steps, lane, grow=len(first) == 2)
                    total = [m + s for m, s in zip(moved, second)]
                    merged.append(total + moved[len(second) :])
                level = merged
                steps *= 2
            for tile, value in enumerate(level[0]):
                bands_ref[tile, pl.ds(i, SUBBANDS, stride=BLOCK), :] = value
            return carry

        lax.fori_loop(0, BLOCK, one_input, 0, unroll=2)
        for tile in range(3):
            out_ref[:, :, tile * LANE : (tile + 1) * LANE] = (
                bands_ref[tile].reshape(SUBBANDS, BLOCK, LANE).astype(jnp.bfloat16)
            )


def filter_bank(samples, taps, table):
    steps = T_DEV // CHUNK
    return pl.pallas_call(
        filter_kernel,
        grid=(steps,),
        in_specs=[
            pl.BlockSpec((BLOCK, CHUNK * BRANCHES), lambda c: (0, c)),
            pl.BlockSpec((TAPS, BRANCHES), lambda c: (0, 0)),
            pl.BlockSpec((SUBBANDS, BRANCHES), lambda c: (0, 0)),
        ],
        out_specs=pl.BlockSpec((SUBBANDS, BLOCK, T_DEV + TAIL), lambda c: (0, 0, 0)),
        out_shape=jax.ShapeDtypeStruct((SUBBANDS, BLOCK, T_DEV + TAIL), jnp.bfloat16),
        scratch_shapes=[
            pltpu.VMEM((2, T_DEV * BLOCK, LANE), jnp.float32),
            pltpu.VMEM((2, TAPS * SUBBANDS, BRANCHES), jnp.bfloat16),
            pltpu.VMEM((3, SUBBANDS * BLOCK, LANE), jnp.float32),
        ],
        compiler_params=pltpu.CompilerParams(vmem_limit_bytes=32 << 20),
        name="filter_bank",
    )(samples, taps, table)


def assemble_kernel(parts_ref, out_ref):
    for core in range(2):
        rows = slice(core * BLOCK, (core + 1) * BLOCK)
        for block in range(N_SUB):
            here = parts_ref[block * 2 + core]
            start = block * T_DEV
            head = here[:, :LANE]
            if block:
                tail = parts_ref[(block - 1) * 2 + core][:, T_DEV:]
                head = (head.astype(jnp.float32) + tail.astype(jnp.float32)).astype(jnp.bfloat16)
            out_ref[rows, start : start + LANE] = head
            out_ref[rows, start + LANE : start + T_DEV] = here[:, LANE:T_DEV]


def assemble(parts):
    return pl.pallas_call(
        assemble_kernel,
        out_shape=jax.ShapeDtypeStruct((2 * BLOCK, TOTAL), jnp.bfloat16),
        name="assemble",
    )(parts)


PAIRS = 4
SPAN = 9 * BLOCK


def build_rows(own_ref, target_ref, slot, first, mask):
    for a in range(2):
        before = None
        for tile in range(TOTAL // LANE + 1):
            row = own_ref[tile, pl.ds(first + a, 1), :]
            rolled = pltpu.roll(
                jnp.broadcast_to(row, (LAGS, LANE)), 0, 1, stride=1, stride_axis=0
            )
            if tile:
                target_ref[slot, a * LAGS : (a + 1) * LAGS, (tile - 1) * LANE : tile * LANE] = (
                    jnp.where(mask, rolled, before).astype(jnp.bfloat16)
                )
            before = rolled


def correlate_kernel(where_ref, *refs):
    blocks = refs[: REACH + 1]
    out_ref, own_ref, span_ref, rows_ref = refs[-4:]
    step = pl.program_id(0)
    row = lax.broadcasted_iota(jnp.int32, (LAGS, LANE), 0)
    mask = lax.broadcasted_iota(jnp.int32, (LAGS, LANE), 1) >= row
    core = where_ref[0]

    @pl.when(step == 0)
    def _():
        offset = pl.multiple_of(core * BLOCK, BLOCK)
        for j in range(REACH + 1):
            size = BLOCK if j == REACH else 2 * BLOCK
            start = 2 * BLOCK * j

            @pl.when(core == 0)
            def _():
                span_ref[start : start + size, :] = blocks[j][:size, :]

            @pl.when(core == 1)
            def _():
                if j == 0:
                    span_ref[:BLOCK, :] = blocks[j][BLOCK:, :]
                else:
                    span_ref[start - BLOCK : start + BLOCK, :] = blocks[j][...]

        own = span_ref[:BLOCK, :].astype(jnp.float32)
        half = jnp.zeros((BLOCK, LAGS // 2), jnp.float32)
        padded = jnp.concatenate([half, own, half], axis=1)
        for tile in range(TOTAL // LANE + 1):
            own_ref[tile] = padded[:, tile * LANE : (tile + 1) * LANE]
        build_rows(own_ref, rows_ref, 0, 0, mask)

    scale = 1.0 / math.sqrt(TOTAL)
    for pair in range(PAIRS):
        index = step * PAIRS + pair
        result = nt_dot(span_ref[...], rows_ref[pair % 2]) * scale
        following = jnp.minimum(index + 1, BLOCK // 2 - 1)
        build_rows(own_ref, rows_ref, (pair + 1) % 2, 2 * following, mask)
        out_ref[0, 2 * pair] = result[:, :LAGS].astype(jnp.bfloat16)
        out_ref[0, 2 * pair + 1] = result[:, LAGS:].astype(jnp.bfloat16)


def correlate(where, blocks, earlier):
    steps = BLOCK // (2 * PAIRS)
    operands = list(blocks)
    in_specs = [pl.BlockSpec((2 * BLOCK, TOTAL), lambda c, w: (0, 0)) for _ in blocks]
    aliases = {}
    if earlier is not None:
        operands.append(earlier)
        in_specs.append(pl.BlockSpec(memory_space=pl.ANY))
        aliases = {len(operands): 0}
    return pl.pallas_call(
        correlate_kernel,
        grid_spec=pltpu.PrefetchScalarGridSpec(
            num_scalar_prefetch=1,
            grid=(steps,),
            in_specs=in_specs,
            out_specs=pl.BlockSpec(
                (1, 2 * PAIRS, SPAN, LAGS), lambda c, w: (w[1], c, 0, 0)
            ),
            scratch_shapes=[
                pltpu.VMEM((TOTAL // LANE + 1, BLOCK, LANE), jnp.float32),
                pltpu.VMEM((SPAN, TOTAL), jnp.bfloat16),
                pltpu.VMEM((2, 2 * LAGS, TOTAL), jnp.bfloat16),
            ],
        ),
        out_shape=jax.ShapeDtypeStruct((2, BLOCK, SPAN, LAGS), jnp.bfloat16),
        input_output_aliases=aliases,
        compiler_params=pltpu.CompilerParams(vmem_limit_bytes=32 << 20),
        name="correlate",
        cost_estimate=pl.CostEstimate(
            flops=2 * BLOCK * SPAN * LAGS * TOTAL, bytes_accessed=4 << 20, transcendentals=0
        ),
    )(where, *operands)


def body(samples, taps):
    core = lax.axis_index("core")
    parts = filter_bank(samples, taps.reshape(TAPS, BRANCHES), cosine_matrix())
    parts = lax.all_to_all(parts, ("sub", "core"), split_axis=0, concat_axis=0, tiled=True)
    mine = assemble(parts)
    held = [mine]
    for step in range(1, REACH + 1):
        pairs = [(source, (source - step) % CHIPS) for source in range(CHIPS)]
        held.append(lax.ppermute(mine, "chip", pairs))
    swapped = [lax.ppermute(value, "core", [(0, 1), (1, 0)]) for value in held]
    first = correlate(jnp.stack([core, core]), held, None)
    return correlate(jnp.stack([core, 1 - core]), swapped, first)


def solution(mesh):
    inner = Mesh(mesh.devices.reshape(N_SUB, CHIPS, 2), ("sub", "chip", "core"))
    in_specs = (P(("chip", "core"), "sub"), P())
    out_specs = P("sub", ("chip", "core"), None, None)
    return jax.shard_map(body, mesh=inner, in_specs=in_specs, out_specs=out_specs, check_vma=False)
```

time: 361 us -> 83.7 us (0.23)
  the two profiles are of different devices: /device:TPU:27 before, /device:TPU:3 now
where the time goes in v1:
time: 83.7 us; the launch traced here: 83.4 us
  Pallas kernels  33.6 us (40%)
  blocking collectives  17.4 us (21%)
  waiting for transfers between devices  14.6 us (17%)
  starting transfers between devices  13.1 us (16%)
  local copies, waits for them, and re-layouts  4.57 us (5%)
    pallas_call x2, Pallas kernels, correlate(): pl.pallas_call(correlate_kernel, grid_spec=pltpu.PrefetchScalarGridSpec(n...  18 us
    all_to_all x1, blocking collectives, body(): lax.all_to_all(parts, ('sub', 'core'), split_axis=0, concat_axis=0, tiled...  17.4 us
    ppermute x4, waiting for transfers between devices, body(): held.append(lax.ppermute(mine, 'chip', pairs))  14.6 us
    pallas_call x1, Pallas kernels, filter_bank(): pl.pallas_call(filter_kernel, grid=(steps,), in_specs=[pl.BlockSpec((BLOC...  13.9 us
    ppermute x4, starting transfers between devices, body(): held.append(lax.ppermute(mine, 'chip', pairs))  6.89 us
    ppermute x5, starting transfers between devices, body(): swapped = [lax.ppermute(value, 'core', [(0, 1), (1, 0)]) for value in held]  6.18 us
    unnamed x6, local copies, waits for them, and re-layouts  3.85 us
    pallas_call x1, Pallas kernels, assemble(): pl.pallas_call(assemble_kernel, out_shape=jax.ShapeDtypeStruct((2 * BLOCK...  1.73 us
  transfers between devices with their start and end apart: 9, of which 2 were waited for; matrix products, arithmetic and copies ran while one was open for 0% of the time, Pallas kernels for 11%

profile of v1, /device:TPU:3, one launch (start us, length us, event | category | flops | bytes accessed | tf_op | source)
XLA Modules:
  0.0 83.4 jit_solution(17368631098603535318)
XLA Ops:
  0.0 0.7 reshape.3.taps_ref
  0.7 0.0 copy-start
  0.7 2.2 %copy-done = bf16[32,65536]{1,0:T(8,128)(2,1)S(1)} copy-done((bf16[32,65536]{1,0:T(8,128)(2,1)S(1)}, bf16[32,65536]{1,0:T(8,128)(2,1)}, u32[]{:S(2)}) %copy-start) | copy-done | bytes 4194328
  2.9 0.0 copy-start.2
  2.9 0.7 copy-done.2
  3.6 13.9 %filter_bank.1 = bf16[16,32,384]{2,1,0:T(8,128)(2,1)S(1)} custom-call(bf16[32,65536]{1,0:T(8,128)(2,1)S(1)} %copy-done, s32[16,256]{1,0:T(8,128)S(1)} %reshape.3.taps_ref, f32[16,256]{1,0:T(8,128)S(1)} %copy-done.2), custom_call_target="tpu_custom_call" | custom-call | tf_op jit(solution)/shard_map/filter_bank/pallas_call | solution.py:105
  17.5 17.4 %all_to_all.5.parts_ref = bf16[16,32,384]{2,1,0:T(8,128)(2,1)} all-to-all(bf16[16,32,384]{2,1,0:T(8,128)(2,1)S(1)} %filter_bank.1), channel_id=1, replica_groups=mesh['sub'=8,'chip'=8,'core'=2] {'sub','core'}, dimensions={0} | all-to-all | bytes 786432 | tf_op jit(solution)/shard_map/all_to_all | solution.py:246
  34.9 1.7 %assemble.1.refs_0_ = bf16[64,2048]{1,0:T(8,128)(2,1)} custom-call(bf16[16,32,384]{2,1,0:T(8,128)(2,1)} %all_to_all.5.parts_ref), custom_call_target="tpu_custom_call" | custom-call | tf_op jit(solution)/shard_map/assemble/pallas_call | solution.py:140
  36.6 2.9 %collective-permute-start.7 = (bf16[64,2048]{1,0:T(8,128)(2,1)}, bf16[64,2048]{1,0:T(8,128)(2,1)S(1)}, u32[]{:S(2)}, u32[]{:S(2)}) collective-permute-start(bf16[64,2048]{1,0:T(8,128)(2,1)} %assemble.1.refs_0_), channel_id=1, source_target_pairs={{0,8},{2,10},{4,12},{6,14},{8,0},{10,2},{12,4},{14,6},{1,9},{3,11}... | collective-permute-start | bytes 786440 | tf_op jit(solution)/shard_map/ppermute | solution.py:251
  39.5 1.6 %collective-permute-start.5 = (bf16[64,2048]{1,0:T(8,128)(2,1)}, bf16[64,2048]{1,0:T(8,128)(2,1)S(1)}, u32[]{:S(2)}, u32[]{:S(2)}) collective-permute-start(bf16[64,2048]{1,0:T(8,128)(2,1)} %assemble.1.refs_0_), channel_id=1, source_target_pairs={{0,10},{2,12},{4,14},{6,0},{8,2},{10,4},{12,6},{14,8},{1,11},{3,13... | collective-permute-start | bytes 786440 | tf_op jit(solution)/shard_map/ppermute | solution.py:251
  41.1 0.0 collective-permute-start.3
  41.1 2.4 %collective-permute-start.1 = (bf16[64,2048]{1,0:T(8,128)(2,1)}, bf16[64,2048]{1,0:T(8,128)(2,1)S(1)}, u32[]{:S(2)}, u32[]{:S(2)}) collective-permute-start(bf16[64,2048]{1,0:T(8,128)(2,1)} %assemble.1.refs_0_), channel_id=1, source_target_pairs={{0,14},{2,0},{4,2},{6,4},{8,6},{10,8},{12,10},{14,12},{1,15},{3,1}... | collective-permute-start | bytes 786440 | tf_op jit(solution)/shard_map/ppermute | solution.py:251
  43.5 0.1 pad_add_fusion
  43.6 2.3 %collective-permute-start = (bf16[64,2048]{1,0:T(8,128)(2,1)}, bf16[64,2048]{1,0:T(8,128)(2,1)S(1)}, u32[]{:S(2)}, u32[]{:S(2)}) collective-permute-start(bf16[64,2048]{1,0:T(8,128)(2,1)} %assemble.1.refs_0_), channel_id=1, source_target_pairs={{0,1},{1,0},{2,3},{3,2},{4,5},{5,4},{6,7},{7,6},{8,9},{9,8},{10,11... | collective-permute-start | bytes 786440 | tf_op jit(solution)/shard_map/ppermute | solution.py:252
  45.9 4.6 %collective-permute-done.7.refs_4_ = bf16[64,2048]{1,0:T(8,128)(2,1)S(1)} collective-permute-done((bf16[64,2048]{1,0:T(8,128)(2,1)}, bf16[64,2048]{1,0:T(8,128)(2,1)S(1)}, u32[]{:S(2)}, u32[]{:S(2)}) %collective-permute-start.7) | collective-permute-done | bytes 262176 | tf_op jit(solution)/shard_map/ppermute | solution.py:251
  50.5 2.0 %collective-permute-start.8 = (bf16[64,2048]{1,0:T(8,128)(2,1)S(1)}, bf16[64,2048]{1,0:T(8,128)(2,1)S(1)}, u32[]{:S(2)}, u32[]{:S(2)}) collective-permute-start(bf16[64,2048]{1,0:T(8,128)(2,1)S(1)} %collective-permute-done.7.refs_4_), channel_id=1, source_target_pairs={{0,1},{1,0},{2,3},{3,2},{4,5},{5,4},{6,7},{7,6},{8,9},{9,8},{10,11... | collective-permute-start | bytes 786440 | tf_op jit(solution)/shard_map/ppermute | solution.py:252
  52.5 0.0 collective-permute-done.5.refs_3_
  52.5 0.3 collective-permute-start.6
  52.8 10.0 %collective-permute-done.3.refs_2_ = bf16[64,2048]{1,0:T(8,128)(2,1)S(1)} collective-permute-done((bf16[64,2048]{1,0:T(8,128)(2,1)}, bf16[64,2048]{1,0:T(8,128)(2,1)S(1)}, u32[]{:S(2)}, u32[]{:S(2)}) %collective-permute-start.3) | collective-permute-done | bytes 262176 | tf_op jit(solution)/shard_map/ppermute | solution.py:251
  62.8 1.5 %collective-permute-start.4 = (bf16[64,2048]{1,0:T(8,128)(2,1)S(1)}, bf16[64,2048]{1,0:T(8,128)(2,1)S(1)}, u32[]{:S(2)}, u32[]{:S(2)}) collective-permute-start(bf16[64,2048]{1,0:T(8,128)(2,1)S(1)} %collective-permute-done.3.refs_2_), channel_id=1, source_target_pairs={{0,1},{1,0},{2,3},{3,2},{4,5},{5,4},{6,7},{7,6},{8,9},{9,8},{10,11... | collective-permute-start | bytes 786440 | tf_op jit(solution)/shard_map/ppermute | solution.py:252
  64.4 0.0 collective-permute-done.1.refs_1_
  64.4 0.0 collective-permute-start.2
  64.4 0.0 copy-start.1
  64.4 0.9 %copy-done.1 = bf16[64,2048]{1,0:T(8,128)(2,1)S(1)} copy-done((bf16[64,2048]{1,0:T(8,128)(2,1)S(1)}, bf16[64,2048]{1,0:T(8,128)(2,1)}, u32[]{:S(2)}) %copy-start.1) | copy-done | bytes 262168
  65.3 9.0 %correlate.2.refs_5_ = bf16[2,32,288,128]{3,2,1,0:T(8,128)(2,1)} custom-call(s32[2]{0:T(128)S(1)} %get-tuple-element.6.where_ref, bf16[64,2048]{1,0:T(8,128)(2,1)S(1)} %copy-done.1, bf16[64,2048]{1,0:T(8,128)(2,1)S(1)} %collective-permute-done.1.refs_1_, bf16[64,2048]{1,0:T(8,128)(2,1)S(1)} %collective-permute-done.3.refs_2_, ...), custom_call_target="tpu_custom_call" | custom-call | flops 4831838208 | bytes 4194304 | tf_op jit(solution)/shard_map/correlate/pallas_call | solution.py:218
  74.3 0.0 collective-permute-done.refs_0_
  74.3 0.0 collective-permute-done.8.refs_4_
  74.3 0.0 collective-permute-done.6.refs_3_
  74.3 0.0 collective-permute-done.4.refs_2_
  74.3 0.0 collective-permute-done.2.refs_1_
  74.4 9.0 %correlate.3 = bf16[2,32,288,128]{3,2,1,0:T(8,128)(2,1)} custom-call(s32[2]{0:T(128)S(1)} %get-tuple-element.5.where_ref, bf16[64,2048]{1,0:T(8,128)(2,1)S(1)} %collective-permute-done.refs_0_, bf16[64,2048]{1,0:T(8,128)(2,1)S(1)} %collective-permute-done.2.refs_1_, ...), custom_call_target="tpu_custom_call", output_to_operand_aliasing={{}: (6, {})} | custom-call | flops 4831838208 | bytes 4194304 | tf_op jit(solution)/shard_map/correlate/pallas_call | solution.py:218
Async XLA Ops:
  0.7 2.2 %copy-start = (bf16[32,65536]{1,0:T(8,128)(2,1)S(1)}, bf16[32,65536]{1,0:T(8,128)(2,1)}, u32[]{:S(2)}) copy-start(bf16[32,65536]{1,0:T(8,128)(2,1)} %x_ref.1) | copy-start | bytes 12582916
  2.9 0.7 copy-start.2
  36.6 13.9 %collective-permute-start.7 = (bf16[64,2048]{1,0:T(8,128)(2,1)}, bf16[64,2048]{1,0:T(8,128)(2,1)S(1)}, u32[]{:S(2)}, u32[]{:S(2)}) collective-permute-start(bf16[64,2048]{1,0:T(8,128)(2,1)} %assemble.1.refs_0_), channel_id=1, source_target_pairs={{0,8},{2,10},{4,12},{6,14},{8,0},{10,2},{12,4},{14,6},{1,9},{3,11}... | collective-permute-start | bytes 786440 | tf_op jit(solution)/shard_map/ppermute | solution.py:251
  39.5 13.0 %collective-permute-start.5 = (bf16[64,2048]{1,0:T(8,128)(2,1)}, bf16[64,2048]{1,0:T(8,128)(2,1)S(1)}, u32[]{:S(2)}, u32[]{:S(2)}) collective-permute-start(bf16[64,2048]{1,0:T(8,128)(2,1)} %assemble.1.refs_0_), channel_id=1, source_target_pairs={{0,10},{2,12},{4,14},{6,0},{8,2},{10,4},{12,6},{14,8},{1,11},{3,13... | collective-permute-start | bytes 786440 | tf_op jit(solution)/shard_map/ppermute | solution.py:251
  41.1 21.7 %collective-permute-start.3 = (bf16[64,2048]{1,0:T(8,128)(2,1)}, bf16[64,2048]{1,0:T(8,128)(2,1)S(1)}, u32[]{:S(2)}, u32[]{:S(2)}) collective-permute-start(bf16[64,2048]{1,0:T(8,128)(2,1)} %assemble.1.refs_0_), channel_id=1, source_target_pairs={{0,12},{2,14},{4,0},{6,2},{8,4},{10,6},{12,8},{14,10},{1,13},{3,15... | collective-permute-start | bytes 786440 | tf_op jit(solution)/shard_map/ppermute | solution.py:251
  41.1 23.2 %collective-permute-start.1 = (bf16[64,2048]{1,0:T(8,128)(2,1)}, bf16[64,2048]{1,0:T(8,128)(2,1)S(1)}, u32[]{:S(2)}, u32[]{:S(2)}) collective-permute-start(bf16[64,2048]{1,0:T(8,128)(2,1)} %assemble.1.refs_0_), channel_id=1, source_target_pairs={{0,14},{2,0},{4,2},{6,4},{8,6},{10,8},{12,10},{14,12},{1,15},{3,1}... | collective-permute-start | bytes 786440 | tf_op jit(solution)/shard_map/ppermute | solution.py:251
  43.6 30.8 %collective-permute-start = (bf16[64,2048]{1,0:T(8,128)(2,1)}, bf16[64,2048]{1,0:T(8,128)(2,1)S(1)}, u32[]{:S(2)}, u32[]{:S(2)}) collective-permute-start(bf16[64,2048]{1,0:T(8,128)(2,1)} %assemble.1.refs_0_), channel_id=1, source_target_pairs={{0,1},{1,0},{2,3},{3,2},{4,5},{5,4},{6,7},{7,6},{8,9},{9,8},{10,11... | collective-permute-start | bytes 786440 | tf_op jit(solution)/shard_map/ppermute | solution.py:252
  50.5 23.9 %collective-permute-start.8 = (bf16[64,2048]{1,0:T(8,128)(2,1)S(1)}, bf16[64,2048]{1,0:T(8,128)(2,1)S(1)}, u32[]{:S(2)}, u32[]{:S(2)}) collective-permute-start(bf16[64,2048]{1,0:T(8,128)(2,1)S(1)} %collective-permute-done.7.refs_4_), channel_id=1, source_target_pairs={{0,1},{1,0},{2,3},{3,2},{4,5},{5,4},{6,7},{7,6},{8,9},{9,8},{10,11... | collective-permute-start | bytes 786440 | tf_op jit(solution)/shard_map/ppermute | solution.py:252
  52.5 21.8 %collective-permute-start.6 = (bf16[64,2048]{1,0:T(8,128)(2,1)S(1)}, bf16[64,2048]{1,0:T(8,128)(2,1)S(1)}, u32[]{:S(2)}, u32[]{:S(2)}) collective-permute-start(bf16[64,2048]{1,0:T(8,128)(2,1)S(1)} %collective-permute-done.5.refs_3_), channel_id=1, source_target_pairs={{0,1},{1,0},{2,3},{3,2},{4,5},{5,4},{6,7},{7,6},{8,9},{9,8},{10,11... | collective-permute-start | bytes 786440 | tf_op jit(solution)/shard_map/ppermute | solution.py:252
  62.8 11.5 %collective-permute-start.4 = (bf16[64,2048]{1,0:T(8,128)(2,1)S(1)}, bf16[64,2048]{1,0:T(8,128)(2,1)S(1)}, u32[]{:S(2)}, u32[]{:S(2)}) collective-permute-start(bf16[64,2048]{1,0:T(8,128)(2,1)S(1)} %collective-permute-done.3.refs_2_), channel_id=1, source_target_pairs={{0,1},{1,0},{2,3},{3,2},{4,5},{5,4},{6,7},{7,6},{8,9},{9,8},{10,11... | collective-permute-start | bytes 786440 | tf_op jit(solution)/shard_map/ppermute | solution.py:252
  64.4 10.0 %collective-permute-start.2 = (bf16[64,2048]{1,0:T(8,128)(2,1)S(1)}, bf16[64,2048]{1,0:T(8,128)(2,1)S(1)}, u32[]{:S(2)}, u32[]{:S(2)}) collective-permute-start(bf16[64,2048]{1,0:T(8,128)(2,1)S(1)} %collective-permute-done.1.refs_1_), channel_id=1, source_target_pairs={{0,1},{1,0},{2,3},{3,2},{4,5},{5,4},{6,7},{7,6},{8,9},{9,8},{10,11... | collective-permute-start | bytes 786440 | tf_op jit(solution)/shard_map/ppermute | solution.py:252
  64.4 0.9 %copy-start.1 = (bf16[64,2048]{1,0:T(8,128)(2,1)S(1)}, bf16[64,2048]{1,0:T(8,128)(2,1)}, u32[]{:S(2)}) copy-start(bf16[64,2048]{1,0:T(8,128)(2,1)} %assemble.1.refs_0_) | copy-start | bytes 786436

commit v2 on v1

--- a/solution.py
+++ b/solution.py
@@ -23,6 +23,7 @@
 CHUNK = 32
 REACH = 4
 LANE = 128
+PITCH = 40
 
 
 def cosine_matrix():
@@ -49,75 +50,92 @@
     return result
 
 
-def filter_kernel(x_ref, taps_ref, cos_ref, out_ref, frames_ref, weight_ref, bands_ref):
-    step = pl.program_id(0)
-    for frame in range(CHUNK):
-        row = pl.multiple_of((step * CHUNK + frame) * BLOCK, BLOCK)
-        for half in range(2):
-            start = frame * BRANCHES + half * LANE
-            frames_ref[half, pl.ds(row, BLOCK), :] = x_ref[:, start : start + LANE].astype(
-                jnp.float32
-            )
-
-    @pl.when(step == pl.num_programs(0) - 1)
-    def _():
-        table = cos_ref[...]
+def filter_kernel(
+    x_hbm, taps_hbm, cos_hbm, out_ref, x_ref, taps_ref, cos_ref, frames_ref, weight_ref, bands_ref, sems
+):
+    def fetch(c):
+        columns = pl.ds(c * CHUNK * BRANCHES, CHUNK * BRANCHES)
+        return pltpu.make_async_copy(x_hbm.at[:, columns], x_ref.at[:, columns], sems.at[c])
+
+    chunks = T_DEV // CHUNK
+    taps_copy = pltpu.make_async_copy(taps_hbm, taps_ref, sems.at[chunks])
+    cos_copy = pltpu.make_async_copy(cos_hbm, cos_ref, sems.at[chunks + 1])
+    taps_copy.start()
+    cos_copy.start()
+    for c in range(chunks):
+        fetch(c).start()
+    taps_copy.wait()
+    cos_copy.wait()
+    table = cos_ref[...]
+    for tap in range(TAPS):
+        coefficients = taps_ref[:, tap * BRANCHES : (tap + 1) * BRANCHES].astype(jnp.float32)
+        product = table * coefficients
+        high = product.astype(jnp.bfloat16)
+        low = (product - high.astype(jnp.float32)).astype(jnp.bfloat16)
+        weight_ref[0, tap * SUBBANDS : (tap + 1) * SUBBANDS, :] = high
+        weight_ref[1, tap * SUBBANDS : (tap + 1) * SUBBANDS, :] = low
+
+    for c in range(chunks):
+        fetch(c).wait()
+
+        def one_frame(frame, carry):
+            row = pl.multiple_of(frame * PITCH, 8)
+            for half in range(2):
+                start = pl.multiple_of(frame * BRANCHES + half * LANE, LANE)
+                frames_ref[half, pl.ds(row, BLOCK), :] = x_ref[:, pl.ds(start, LANE)].astype(
+                    jnp.float32
+                )
+            return carry
+
+        lax.fori_loop(c * CHUNK, (c + 1) * CHUNK, one_frame, 0, unroll=8)
+
+    lane = lax.broadcasted_iota(jnp.int32, (SUBBANDS, LANE), 1)
+
+    def one_input(i, carry):
+        data = jnp.concatenate(
+            [frames_ref[half, pl.ds(i, T_DEV, stride=PITCH), :] for half in range(2)], axis=1
+        ).astype(jnp.bfloat16)
+        products = nt_dot(weight_ref[0], data) + nt_dot(weight_ref[1], data)
+        level = []
         for tap in range(TAPS):
-            product = table * taps_ref[tap : tap + 1, :].astype(jnp.float32)
-            high = product.astype(jnp.bfloat16)
-            low = (product - high.astype(jnp.float32)).astype(jnp.bfloat16)
-            weight_ref[0, tap * SUBBANDS : (tap + 1) * SUBBANDS, :] = high
-            weight_ref[1, tap * SUBBANDS : (tap + 1) * SUBBANDS, :] = low
-
-        lane = lax.broadcasted_iota(jnp.int32, (SUBBANDS, LANE), 1)
-
-        def one_input(i, carry):
-            data = jnp.concatenate(
-                [frames_ref[half, pl.ds(i, T_DEV, stride=BLOCK), :] for half in range(2)], axis=1
-            ).astype(jnp.bfloat16)
-            products = nt_dot(weight_ref[0], data) + nt_dot(weight_ref[1], data)
-            level = []
-            for tap in range(TAPS):
-                part = products[tap * SUBBANDS : (tap + 1) * SUBBANDS]
-                level.append([part[:, :LANE], part[:, LANE:]])
-            steps = 1
-            while len(level) > 1:
-                merged = []
-                for first, second in zip(level[0::2], level[1::2]):
-                    moved = shift_lanes(first, steps, lane, grow=len(first) == 2)
-                    total = [m + s for m, s in zip(moved, second)]
-                    merged.append(total + moved[len(second) :])
-                level = merged
-                steps *= 2
-            for tile, value in enumerate(level[0]):
-                bands_ref[tile, pl.ds(i, SUBBANDS, stride=BLOCK), :] = value
-            return carry
-
-        lax.fori_loop(0, BLOCK, one_input, 0, unroll=2)
-        for tile in range(3):
-            out_ref[:, :, tile * LANE : (tile + 1) * LANE] = (
-                bands_ref[tile].reshape(SUBBANDS, BLOCK, LANE).astype(jnp.bfloat16)
-            )
+            part = products[tap * SUBBANDS : (tap + 1) * SUBBANDS]
+            level.append([part[:, :LANE], part[:, LANE:]])
+        steps = 1
+        while len(level) > 1:
+            merged = []
+            for first, second in zip(level[0::2], level[1::2]):
+                moved = shift_lanes(first, steps, lane, grow=len(first) == 2)
+                total = [m + s for m, s in zip(moved, second)]
+                merged.append(total + moved[len(second) :])
+            level = merged
+            steps *= 2
+        for tile, value in enumerate(level[0]):
+            bands_ref[tile, pl.ds(i, SUBBANDS, stride=PITCH), :] = value
+        return carry
+
+    lax.fori_loop(0, BLOCK, one_input, 0, unroll=16)
+    for tile in range(3):
+        out_ref[:, :, tile * LANE : (tile + 1) * LANE] = (
+            bands_ref[tile].reshape(SUBBANDS, PITCH, LANE)[:, :BLOCK].astype(jnp.bfloat16)
+        )
 
 
 def filter_bank(samples, taps, table):
-    steps = T_DEV // CHUNK
     return pl.pallas_call(
         filter_kernel,
-        grid=(steps,),
-        in_specs=[
-            pl.BlockSpec((BLOCK, CHUNK * BRANCHES), lambda c: (0, c)),
-            pl.BlockSpec((TAPS, BRANCHES), lambda c: (0, 0)),
-            pl.BlockSpec((SUBBANDS, BRANCHES), lambda c: (0, 0)),
-        ],
-        out_specs=pl.BlockSpec((SUBBANDS, BLOCK, T_DEV + TAIL), lambda c: (0, 0, 0)),
+        in_specs=[pl.BlockSpec(memory_space=pl.ANY)] * 3,
+        out_specs=pl.BlockSpec(memory_space=pltpu.VMEM),
         out_shape=jax.ShapeDtypeStruct((SUBBANDS, BLOCK, T_DEV + TAIL), jnp.bfloat16),
         scratch_shapes=[
-            pltpu.VMEM((2, T_DEV * BLOCK, LANE), jnp.float32),
+            pltpu.VMEM((BLOCK, T_DEV * BRANCHES), jnp.bfloat16),
+            pltpu.VMEM((1, TAPS * BRANCHES), jnp.int32),
+            pltpu.VMEM((SUBBANDS, BRANCHES), jnp.float32),
+            pltpu.VMEM((2, T_DEV * PITCH, LANE), jnp.float32),
             pltpu.VMEM((2, TAPS * SUBBANDS, BRANCHES), jnp.bfloat16),
-            pltpu.VMEM((3, SUBBANDS * BLOCK, LANE), jnp.float32),
+            pltpu.VMEM((3, SUBBANDS * PITCH, LANE), jnp.float32),
+            pltpu.SemaphoreType.DMA((T_DEV // CHUNK + 2,)),
         ],
-        compiler_params=pltpu.CompilerParams(vmem_limit_bytes=32 << 20),
+        compiler_params=pltpu.CompilerParams(vmem_limit_bytes=60 << 20),
         name="filter_bank",
     )(samples, taps, table)
 
@@ -242,7 +260,7 @@
 
 def body(samples, taps):
     core = lax.axis_index("core")
-    parts = filter_bank(samples, taps.reshape(TAPS, BRANCHES), cosine_matrix())
+    parts = filter_bank(samples, taps[None], cosine_matrix())
     parts = lax.all_to_all(parts, ("sub", "core"), split_axis=0, concat_axis=0, tiled=True)
     mine = assemble(parts)
     held = [mine]

time: 83.7 us -> 73.5 us (0.88)
  Pallas kernels: 33.6 us -> 27 us
  local copies, waits for them, and re-layouts: 4.57 us -> 0.95 us
    pallas_call x1, Pallas kernels: 13.9 us -> 7.19 us  [filter_bank(): pl.pallas_call(filter_kernel, in_specs=[pl.BlockSpec(memory_space=pl.ANY)...]
    unnamed x6 -> x2, local copies, waits for them, and re-layouts: 3.85 us -> 0.95 us
  transfers between devices with their start and end apart: 9 -> 9, of which waited for: 2 -> 2; matrix products, arithmetic and copies ran while one was open for 0% -> 0% of each run, Pallas kernels for 11% -> 12%
where the time goes in v2:
time: 73.5 us; the launch traced here: 73.3 us
  Pallas kernels  27 us (37%)
  blocking collectives  17.6 us (24%)
  waiting for transfers between devices  14.6 us (20%)
  starting transfers between devices  13.1 us (18%)
  local copies, waits for them, and re-layouts  0.95 us (1%)
    pallas_call x2, Pallas kernels, correlate(): pl.pallas_call(correlate_kernel, grid_spec=pltpu.PrefetchScalarGridSpec(n...  18 us
    all_to_all x1, blocking collectives, body(): lax.all_to_all(parts, ('sub', 'core'), split_axis=0, concat_axis=0, tiled...  17.6 us
    ppermute x4, waiting for transfers between devices, body(): held.append(lax.ppermute(mine, 'chip', pairs))  14.6 us
    pallas_call x1, Pallas kernels, filter_bank(): pl.pallas_call(filter_kernel, in_specs=[pl.BlockSpec(memory_space=pl.ANY)...  7.19 us
    ppermute x4, starting transfers between devices, body(): held.append(lax.ppermute(mine, 'chip', pairs))  6.89 us
    ppermute x5, starting transfers between devices, body(): swapped = [lax.ppermute(value, 'core', [(0, 1), (1, 0)]) for value in held]  6.18 us
    pallas_call x1, Pallas kernels, assemble(): pl.pallas_call(assemble_kernel, out_shape=jax.ShapeDtypeStruct((2 * BLOCK...  1.73 us
  transfers between devices with their start and end apart: 9, of which 2 were waited for; matrix products, arithmetic and copies ran while one was open for 0% of the time, Pallas kernels for 12%

profile of v2, /device:TPU:3, one launch (start us, length us, event | category | flops | bytes accessed | tf_op | source)
XLA Modules:
  0.0 73.3 jit_solution(15654334645784673568)
XLA Ops:
  0.0 7.2 %filter_bank.1 = bf16[16,32,384]{2,1,0:T(8,128)(2,1)} custom-call(bf16[32,65536]{1,0:T(8,128)(2,1)} %x_hbm.1, s32[1,4096]{1,0:T(1,128)} %bitcast.3, f32[16,256]{1,0:T(8,128)} %constant.10.cos_hbm), custom_call_target="tpu_custom_call" | custom-call | tf_op jit(solution)/shard_map/filter_bank/pallas_call | solution.py:124
  7.2 17.6 %all_to_all.5.parts_ref = bf16[16,32,384]{2,1,0:T(8,128)(2,1)} all-to-all(bf16[16,32,384]{2,1,0:T(8,128)(2,1)} %filter_bank.1), channel_id=1, replica_groups=mesh['sub'=8,'chip'=8,'core'=2] {'sub','core'}, dimensions={0} | all-to-all | bytes 786432 | tf_op jit(solution)/shard_map/all_to_all | solution.py:264
  24.8 1.7 %assemble.1.refs_0_ = bf16[64,2048]{1,0:T(8,128)(2,1)} custom-call(bf16[16,32,384]{2,1,0:T(8,128)(2,1)} %all_to_all.5.parts_ref), custom_call_target="tpu_custom_call" | custom-call | tf_op jit(solution)/shard_map/assemble/pallas_call | solution.py:158
  26.5 2.9 %collective-permute-start.7 = (bf16[64,2048]{1,0:T(8,128)(2,1)}, bf16[64,2048]{1,0:T(8,128)(2,1)S(1)}, u32[]{:S(2)}, u32[]{:S(2)}) collective-permute-start(bf16[64,2048]{1,0:T(8,128)(2,1)} %assemble.1.refs_0_), channel_id=1, source_target_pairs={{0,8},{2,10},{4,12},{6,14},{8,0},{10,2},{12,4},{14,6},{1,9},{3,11}... | collective-permute-start | bytes 786440 | tf_op jit(solution)/shard_map/ppermute | solution.py:269
  29.4 1.6 %collective-permute-start.5 = (bf16[64,2048]{1,0:T(8,128)(2,1)}, bf16[64,2048]{1,0:T(8,128)(2,1)S(1)}, u32[]{:S(2)}, u32[]{:S(2)}) collective-permute-start(bf16[64,2048]{1,0:T(8,128)(2,1)} %assemble.1.refs_0_), channel_id=1, source_target_pairs={{0,10},{2,12},{4,14},{6,0},{8,2},{10,4},{12,6},{14,8},{1,11},{3,13... | collective-permute-start | bytes 786440 | tf_op jit(solution)/shard_map/ppermute | solution.py:269
  31.0 0.0 collective-permute-start.3
  31.0 2.3 %collective-permute-start.1 = (bf16[64,2048]{1,0:T(8,128)(2,1)}, bf16[64,2048]{1,0:T(8,128)(2,1)S(1)}, u32[]{:S(2)}, u32[]{:S(2)}) collective-permute-start(bf16[64,2048]{1,0:T(8,128)(2,1)} %assemble.1.refs_0_), channel_id=1, source_target_pairs={{0,14},{2,0},{4,2},{6,4},{8,6},{10,8},{12,10},{14,12},{1,15},{3,1}... | collective-permute-start | bytes 786440 | tf_op jit(solution)/shard_map/ppermute | solution.py:269
  33.4 0.1 pad_add_fusion
  33.5 2.3 %collective-permute-start = (bf16[64,2048]{1,0:T(8,128)(2,1)}, bf16[64,2048]{1,0:T(8,128)(2,1)S(1)}, u32[]{:S(2)}, u32[]{:S(2)}) collective-permute-start(bf16[64,2048]{1,0:T(8,128)(2,1)} %assemble.1.refs_0_), channel_id=1, source_target_pairs={{0,1},{1,0},{2,3},{3,2},{4,5},{5,4},{6,7},{7,6},{8,9},{9,8},{10,11... | collective-permute-start | bytes 786440 | tf_op jit(solution)/shard_map/ppermute | solution.py:270
  35.8 4.6 %collective-permute-done.7.refs_4_ = bf16[64,2048]{1,0:T(8,128)(2,1)S(1)} collective-permute-done((bf16[64,2048]{1,0:T(8,128)(2,1)}, bf16[64,2048]{1,0:T(8,128)(2,1)S(1)}, u32[]{:S(2)}, u32[]{:S(2)}) %collective-permute-start.7) | collective-permute-done | bytes 262176 | tf_op jit(solution)/shard_map/ppermute | solution.py:269
  40.4 2.0 %collective-permute-start.8 = (bf16[64,2048]{1,0:T(8,128)(2,1)S(1)}, bf16[64,2048]{1,0:T(8,128)(2,1)S(1)}, u32[]{:S(2)}, u32[]{:S(2)}) collective-permute-start(bf16[64,2048]{1,0:T(8,128)(2,1)S(1)} %collective-permute-done.7.refs_4_), channel_id=1, source_target_pairs={{0,1},{1,0},{2,3},{3,2},{4,5},{5,4},{6,7},{7,6},{8,9},{9,8},{10,11... | collective-permute-start | bytes 786440 | tf_op jit(solution)/shard_map/ppermute | solution.py:270
  42.4 0.0 collective-permute-done.5.refs_3_
  42.4 0.4 collective-permute-start.6
  42.7 10.0 %collective-permute-done.3.refs_2_ = bf16[64,2048]{1,0:T(8,128)(2,1)S(1)} collective-permute-done((bf16[64,2048]{1,0:T(8,128)(2,1)}, bf16[64,2048]{1,0:T(8,128)(2,1)S(1)}, u32[]{:S(2)}, u32[]{:S(2)}) %collective-permute-start.3) | collective-permute-done | bytes 262176 | tf_op jit(solution)/shard_map/ppermute | solution.py:269
  52.7 1.5 %collective-permute-start.4 = (bf16[64,2048]{1,0:T(8,128)(2,1)S(1)}, bf16[64,2048]{1,0:T(8,128)(2,1)S(1)}, u32[]{:S(2)}, u32[]{:S(2)}) collective-permute-start(bf16[64,2048]{1,0:T(8,128)(2,1)S(1)} %collective-permute-done.3.refs_2_), channel_id=1, source_target_pairs={{0,1},{1,0},{2,3},{3,2},{4,5},{5,4},{6,7},{7,6},{8,9},{9,8},{10,11... | collective-permute-start | bytes 786440 | tf_op jit(solution)/shard_map/ppermute | solution.py:270
  54.2 0.0 collective-permute-done.1.refs_1_
  54.2 0.0 collective-permute-start.2
  54.2 0.0 copy-start
  54.2 0.9 %copy-done = bf16[64,2048]{1,0:T(8,128)(2,1)S(1)} copy-done((bf16[64,2048]{1,0:T(8,128)(2,1)S(1)}, bf16[64,2048]{1,0:T(8,128)(2,1)}, u32[]{:S(2)}) %copy-start) | copy-done | bytes 262168
  55.2 9.0 %correlate.2.refs_5_ = bf16[2,32,288,128]{3,2,1,0:T(8,128)(2,1)} custom-call(s32[2]{0:T(128)S(1)} %get-tuple-element.6.where_ref, bf16[64,2048]{1,0:T(8,128)(2,1)S(1)} %copy-done, bf16[64,2048]{1,0:T(8,128)(2,1)S(1)} %collective-permute-done.1.refs_1_, bf16[64,2048]{1,0:T(8,128)(2,1)S(1)} %collective-permute-done.3.refs_2_, ...), custom_call_target="tpu_custom_call" | custom-call | flops 4831838208 | bytes 4194304 | tf_op jit(solution)/shard_map/correlate/pallas_call | solution.py:236
  64.2 0.0 collective-permute-done.refs_0_
  64.2 0.0 collective-permute-done.8.refs_4_
  64.2 0.0 collective-permute-done.6.refs_3_
  64.2 0.0 collective-permute-done.4.refs_2_
  64.2 0.0 collective-permute-done.2.refs_1_
  64.2 9.0 %correlate.3 = bf16[2,32,288,128]{3,2,1,0:T(8,128)(2,1)} custom-call(s32[2]{0:T(128)S(1)} %get-tuple-element.5.where_ref, bf16[64,2048]{1,0:T(8,128)(2,1)S(1)} %collective-permute-done.refs_0_, bf16[64,2048]{1,0:T(8,128)(2,1)S(1)} %collective-permute-done.2.refs_1_, ...), custom_call_target="tpu_custom_call", output_to_operand_aliasing={{}: (6, {})} | custom-call | flops 4831838208 | bytes 4194304 | tf_op jit(solution)/shard_map/correlate/pallas_call | solution.py:236
Async XLA Ops:
  26.5 13.9 %collective-permute-start.7 = (bf16[64,2048]{1,0:T(8,128)(2,1)}, bf16[64,2048]{1,0:T(8,128)(2,1)S(1)}, u32[]{:S(2)}, u32[]{:S(2)}) collective-permute-start(bf16[64,2048]{1,0:T(8,128)(2,1)} %assemble.1.refs_0_), channel_id=1, source_target_pairs={{0,8},{2,10},{4,12},{6,14},{8,0},{10,2},{12,4},{14,6},{1,9},{3,11}... | collective-permute-start | bytes 786440 | tf_op jit(solution)/shard_map/ppermute | solution.py:269
  29.4 13.0 %collective-permute-start.5 = (bf16[64,2048]{1,0:T(8,128)(2,1)}, bf16[64,2048]{1,0:T(8,128)(2,1)S(1)}, u32[]{:S(2)}, u32[]{:S(2)}) collective-permute-start(bf16[64,2048]{1,0:T(8,128)(2,1)} %assemble.1.refs_0_), channel_id=1, source_target_pairs={{0,10},{2,12},{4,14},{6,0},{8,2},{10,4},{12,6},{14,8},{1,11},{3,13... | collective-permute-start | bytes 786440 | tf_op jit(solution)/shard_map/ppermute | solution.py:269
  31.0 21.7 %collective-permute-start.3 = (bf16[64,2048]{1,0:T(8,128)(2,1)}, bf16[64,2048]{1,0:T(8,128)(2,1)S(1)}, u32[]{:S(2)}, u32[]{:S(2)}) collective-permute-start(bf16[64,2048]{1,0:T(8,128)(2,1)} %assemble.1.refs_0_), channel_id=1, source_target_pairs={{0,12},{2,14},{4,0},{6,2},{8,4},{10,6},{12,8},{14,10},{1,13},{3,15... | collective-permute-start | bytes 786440 | tf_op jit(solution)/shard_map/ppermute | solution.py:269
  31.0 23.2 %collective-permute-start.1 = (bf16[64,2048]{1,0:T(8,128)(2,1)}, bf16[64,2048]{1,0:T(8,128)(2,1)S(1)}, u32[]{:S(2)}, u32[]{:S(2)}) collective-permute-start(bf16[64,2048]{1,0:T(8,128)(2,1)} %assemble.1.refs_0_), channel_id=1, source_target_pairs={{0,14},{2,0},{4,2},{6,4},{8,6},{10,8},{12,10},{14,12},{1,15},{3,1}... | collective-permute-start | bytes 786440 | tf_op jit(solution)/shard_map/ppermute | solution.py:269
  33.5 30.7 %collective-permute-start = (bf16[64,2048]{1,0:T(8,128)(2,1)}, bf16[64,2048]{1,0:T(8,128)(2,1)S(1)}, u32[]{:S(2)}, u32[]{:S(2)}) collective-permute-start(bf16[64,2048]{1,0:T(8,128)(2,1)} %assemble.1.refs_0_), channel_id=1, source_target_pairs={{0,1},{1,0},{2,3},{3,2},{4,5},{5,4},{6,7},{7,6},{8,9},{9,8},{10,11... | collective-permute-start | bytes 786440 | tf_op jit(solution)/shard_map/ppermute | solution.py:270
  40.4 23.9 %collective-permute-start.8 = (bf16[64,2048]{1,0:T(8,128)(2,1)S(1)}, bf16[64,2048]{1,0:T(8,128)(2,1)S(1)}, u32[]{:S(2)}, u32[]{:S(2)}) collective-permute-start(bf16[64,2048]{1,0:T(8,128)(2,1)S(1)} %collective-permute-done.7.refs_4_), channel_id=1, source_target_pairs={{0,1},{1,0},{2,3},{3,2},{4,5},{5,4},{6,7},{7,6},{8,9},{9,8},{10,11... | collective-permute-start | bytes 786440 | tf_op jit(solution)/shard_map/ppermute | solution.py:270
  42.4 21.8 %collective-permute-start.6 = (bf16[64,2048]{1,0:T(8,128)(2,1)S(1)}, bf16[64,2048]{1,0:T(8,128)(2,1)S(1)}, u32[]{:S(2)}, u32[]{:S(2)}) collective-permute-start(bf16[64,2048]{1,0:T(8,128)(2,1)S(1)} %collective-permute-done.5.refs_3_), channel_id=1, source_target_pairs={{0,1},{1,0},{2,3},{3,2},{4,5},{5,4},{6,7},{7,6},{8,9},{9,8},{10,11... | collective-permute-start | bytes 786440 | tf_op jit(solution)/shard_map/ppermute | solution.py:270
  52.7 11.5 %collective-permute-start.4 = (bf16[64,2048]{1,0:T(8,128)(2,1)S(1)}, bf16[64,2048]{1,0:T(8,128)(2,1)S(1)}, u32[]{:S(2)}, u32[]{:S(2)}) collective-permute-start(bf16[64,2048]{1,0:T(8,128)(2,1)S(1)} %collective-permute-done.3.refs_2_), channel_id=1, source_target_pairs={{0,1},{1,0},{2,3},{3,2},{4,5},{5,4},{6,7},{7,6},{8,9},{9,8},{10,11... | collective-permute-start | bytes 786440 | tf_op jit(solution)/shard_map/ppermute | solution.py:270
  54.2 10.0 %collective-permute-start.2 = (bf16[64,2048]{1,0:T(8,128)(2,1)S(1)}, bf16[64,2048]{1,0:T(8,128)(2,1)S(1)}, u32[]{:S(2)}, u32[]{:S(2)}) collective-permute-start(bf16[64,2048]{1,0:T(8,128)(2,1)S(1)} %collective-permute-done.1.refs_1_), channel_id=1, source_target_pairs={{0,1},{1,0},{2,3},{3,2},{4,5},{5,4},{6,7},{7,6},{8,9},{9,8},{10,11... | collective-permute-start | bytes 786440 | tf_op jit(solution)/shard_map/ppermute | solution.py:270
  54.2 0.9 %copy-start = (bf16[64,2048]{1,0:T(8,128)(2,1)S(1)}, bf16[64,2048]{1,0:T(8,128)(2,1)}, u32[]{:S(2)}) copy-start(bf16[64,2048]{1,0:T(8,128)(2,1)} %assemble.1.refs_0_) | copy-start | bytes 786436

commit v3 on v2

--- a/solution.py
+++ b/solution.py
@@ -17,7 +17,7 @@
 SUBBANDS = 16
 BLOCK = 32
 N_SUB = 8
-CHIPS = 8
+ROWS = 4
 TOTAL = T_DEV * N_SUB
 TAIL = 128
 CHUNK = 32
@@ -162,7 +162,7 @@
     )(parts)
 
 
-PAIRS = 4
+PAIRS = 8
 SPAN = 9 * BLOCK
 
 
@@ -181,31 +181,54 @@
             before = rolled
 
 
-def correlate_kernel(where_ref, *refs):
-    blocks = refs[: REACH + 1]
-    out_ref, own_ref, span_ref, rows_ref = refs[-4:]
-    step = pl.program_id(0)
+HELD = 6
+
+
+def chip_source(j, column):
+    return {1: (3, 4), 2: (1, 1), 3: (4, 5), 4: (2, 2)}[j][column]
+
+
+def correlate_kernel(core_ref, column_ref, *refs):
+    count = HELD
+    straight, crossed = refs[:count], refs[count : 2 * count]
+    out_ref, own_ref, span_ref, rows_ref, mine_ref, sems = refs[2 * count :]
+    band = pl.program_id(0)
+    step = pl.program_id(1)
     row = lax.broadcasted_iota(jnp.int32, (LAGS, LANE), 0)
     mask = lax.broadcasted_iota(jnp.int32, (LAGS, LANE), 1) >= row
-    core = where_ref[0]
-
-    @pl.when(step == 0)
-    def _():
-        offset = pl.multiple_of(core * BLOCK, BLOCK)
-        for j in range(REACH + 1):
+    core = core_ref[0]
+    column = column_ref[0]
+
+    def gather(blocks, base):
+        first = pltpu.make_async_copy(base, mine_ref, sems.at[0])
+        first.start()
+        for j in range(1, REACH + 1):
             size = BLOCK if j == REACH else 2 * BLOCK
             start = 2 * BLOCK * j
 
-            @pl.when(core == 0)
-            def _():
-                span_ref[start : start + size, :] = blocks[j][:size, :]
-
-            @pl.when(core == 1)
-            def _():
-                if j == 0:
-                    span_ref[:BLOCK, :] = blocks[j][BLOCK:, :]
-                else:
-                    span_ref[start - BLOCK : start + BLOCK, :] = blocks[j][...]
+            columns = {}
+            for number in range(2):
+                columns.setdefault(chip_source(j, number), []).append(number)
+            for source, which in columns.items():
+                here = (column >= which[0]) & (column <= which[-1])
+
+                @pl.when(here & (core == 0))
+                def _():
+                    span_ref[start : start + size, :] = blocks[source][:size, :]
+
+                @pl.when(here & (core == 1))
+                def _():
+                    span_ref[start - BLOCK : start + BLOCK, :] = blocks[source][...]
+
+        first.wait()
+
+        @pl.when(core == 0)
+        def _():
+            span_ref[: 2 * BLOCK, :] = mine_ref[...]
+
+        @pl.when(core == 1)
+        def _():
+            span_ref[:BLOCK, :] = mine_ref[BLOCK:, :]
 
         own = span_ref[:BLOCK, :].astype(jnp.float32)
         half = jnp.zeros((BLOCK, LAGS // 2), jnp.float32)
@@ -213,6 +236,14 @@
         for tile in range(TOTAL // LANE + 1):
             own_ref[tile] = padded[:, tile * LANE : (tile + 1) * LANE]
         build_rows(own_ref, rows_ref, 0, 0, mask)
+
+    @pl.when(jnp.logical_and(step == 0, band == 0))
+    def _():
+        gather(straight, straight[0])
+
+    @pl.when(jnp.logical_and(step == 0, band == 1))
+    def _():
+        gather(crossed, crossed[0])
 
     scale = 1.0 / math.sqrt(TOTAL)
     for pair in range(PAIRS):
@@ -224,38 +255,39 @@
         out_ref[0, 2 * pair + 1] = result[:, LAGS:].astype(jnp.bfloat16)
 
 
-def correlate(where, blocks, earlier):
+def correlate(core, column, straight, crossed):
     steps = BLOCK // (2 * PAIRS)
-    operands = list(blocks)
-    in_specs = [pl.BlockSpec((2 * BLOCK, TOTAL), lambda c, w: (0, 0)) for _ in blocks]
-    aliases = {}
-    if earlier is not None:
-        operands.append(earlier)
-        in_specs.append(pl.BlockSpec(memory_space=pl.ANY))
-        aliases = {len(operands): 0}
+    held = pl.BlockSpec(memory_space=pltpu.VMEM)
+    anywhere = pl.BlockSpec(memory_space=pl.ANY)
     return pl.pallas_call(
         correlate_kernel,
         grid_spec=pltpu.PrefetchScalarGridSpec(
-            num_scalar_prefetch=1,
-            grid=(steps,),
-            in_specs=in_specs,
+            num_scalar_prefetch=2,
+            grid=(2, steps),
+            in_specs=([anywhere] + [held] * (HELD - 1)) * 2,
             out_specs=pl.BlockSpec(
-                (1, 2 * PAIRS, SPAN, LAGS), lambda c, w: (w[1], c, 0, 0)
+                (1, 2 * PAIRS, SPAN, LAGS), lambda s, c, w, v: (lax.rem(w[0] + s, 2), c, 0, 0)
             ),
             scratch_shapes=[
                 pltpu.VMEM((TOTAL // LANE + 1, BLOCK, LANE), jnp.float32),
                 pltpu.VMEM((SPAN, TOTAL), jnp.bfloat16),
                 pltpu.VMEM((2, 2 * LAGS, TOTAL), jnp.bfloat16),
+                pltpu.VMEM((2 * BLOCK, TOTAL), jnp.bfloat16),
+                pltpu.SemaphoreType.DMA((1,)),
             ],
         ),
         out_shape=jax.ShapeDtypeStruct((2, BLOCK, SPAN, LAGS), jnp.bfloat16),
-        input_output_aliases=aliases,
         compiler_params=pltpu.CompilerParams(vmem_limit_bytes=32 << 20),
         name="correlate",
         cost_estimate=pl.CostEstimate(
-            flops=2 * BLOCK * SPAN * LAGS * TOTAL, bytes_accessed=4 << 20, transcendentals=0
+            flops=4 * BLOCK * SPAN * LAGS * TOTAL, bytes_accessed=8 << 20, transcendentals=0
         ),
-    )(where, *operands)
+    )(core, column, *straight, *crossed)
+
+
+def up(value, steps):
+    pairs = [(source, (source - steps) % ROWS) for source in range(ROWS)]
+    return lax.ppermute(value, "row", pairs)
 
 
 def body(samples, taps):
@@ -263,17 +295,23 @@
     parts = filter_bank(samples, taps[None], cosine_matrix())
     parts = lax.all_to_all(parts, ("sub", "core"), split_axis=0, concat_axis=0, tiled=True)
     mine = assemble(parts)
-    held = [mine]
-    for step in range(1, REACH + 1):
-        pairs = [(source, (source - step) % CHIPS) for source in range(CHIPS)]
-        held.append(lax.ppermute(mine, "chip", pairs))
+    above, second = up(mine, 1), up(mine, 2)
+    held = [
+        mine,
+        above,
+        second,
+        lax.ppermute(mine, "column", [(1, 0)]),
+        lax.ppermute(above, "column", [(0, 1), (1, 0)]),
+        lax.ppermute(second, "column", [(0, 1)]),
+    ]
     swapped = [lax.ppermute(value, "core", [(0, 1), (1, 0)]) for value in held]
-    first = correlate(jnp.stack([core, core]), held, None)
-    return correlate(jnp.stack([core, 1 - core]), swapped, first)
+    column = lax.axis_index("column")
+    return correlate(core[None], column[None], held, swapped)
 
 
 def solution(mesh):
-    inner = Mesh(mesh.devices.reshape(N_SUB, CHIPS, 2), ("sub", "chip", "core"))
-    in_specs = (P(("chip", "core"), "sub"), P())
-    out_specs = P("sub", ("chip", "core"), None, None)
+    inner = Mesh(mesh.devices.reshape(N_SUB, ROWS, 2, 2), ("sub", "row", "column", "core"))
+    stations = ("row", "column", "core")
+    in_specs = (P(stations, "sub"), P())
+    out_specs = P("sub", stations, None, None)
     return jax.shard_map(body, mesh=inner, in_specs=in_specs, out_specs=out_specs, check_vma=False)

time: 73.5 us -> 70 us (0.952)
  the two profiles are of different devices: /device:TPU:3 before, /device:TPU:27 now
where the time goes in v3:
time: 70 us; the launch traced here: 69.7 us
  Pallas kernels  24 us (34%)
  blocking collectives  17.6 us (25%)
  starting transfers between devices  15.5 us (22%)
  waiting for transfers between devices  11.7 us (17%)
  local copies, waits for them, and re-layouts  0.95 us (1%)
    all_to_all x1, blocking collectives, body(): lax.all_to_all(parts, ('sub', 'core'), split_axis=0, concat_axis=0, tiled...  17.6 us
    pallas_call x1, Pallas kernels, correlate(): pl.pallas_call(correlate_kernel, grid_spec=pltpu.PrefetchScalarGridSpec(n...  15.1 us
    ppermute x6, starting transfers between devices, body(): swapped = [lax.ppermute(value, 'core', [(0, 1), (1, 0)]) for value in held]  9.06 us
    ppermute x2, waiting for transfers between devices, up(): return lax.ppermute(value, 'row', pairs)  8.81 us
    pallas_call x1, Pallas kernels, filter_bank(): pl.pallas_call(filter_kernel, in_specs=[pl.BlockSpec(memory_space=pl.ANY)...  7.18 us
    ppermute x1, starting transfers between devices, body(): lax.ppermute(mine, 'column', [(1, 0)])  3.06 us
    pallas_call x1, Pallas kernels, assemble(): pl.pallas_call(assemble_kernel, out_shape=jax.ShapeDtypeStruct((2 * BLOCK...  1.74 us
    ppermute x1, waiting for transfers between devices, body(): lax.ppermute(above, 'column', [(0, 1), (1, 0)])  1.72 us
  transfers between devices with their start and end apart: 11, of which 4 were waited for; matrix products, arithmetic and copies ran while one was open for 0% of the time, Pallas kernels for 0%

profile of v3, /device:TPU:27, one launch (start us, length us, event | category | flops | bytes accessed | tf_op | source)
XLA Modules:
  0.0 69.7 jit_solution(11713505636204399690)
XLA Ops:
  0.0 7.2 %filter_bank.1 = bf16[16,32,384]{2,1,0:T(8,128)(2,1)} custom-call(bf16[32,65536]{1,0:T(8,128)(2,1)} %x_hbm.1, s32[1,4096]{1,0:T(1,128)} %bitcast.3, f32[16,256]{1,0:T(8,128)} %constant.10.cos_hbm), custom_call_target="tpu_custom_call" | custom-call | tf_op jit(solution)/shard_map/filter_bank/pallas_call | solution.py:124
  7.2 17.6 %all_to_all.5.parts_ref = bf16[16,32,384]{2,1,0:T(8,128)(2,1)} all-to-all(bf16[16,32,384]{2,1,0:T(8,128)(2,1)} %filter_bank.1), channel_id=1, replica_groups=mesh['sub'=8,'row'=4,'column'=2,'core'=2] {'sub','core'}, dimensions={0} | all-to-all | bytes 786432 | tf_op jit(solution)/shard_map/all_to_all | solution.py:296
  24.8 1.7 %assemble.1.refs_0_ = bf16[64,2048]{1,0:T(8,128)(2,1)} custom-call(bf16[16,32,384]{2,1,0:T(8,128)(2,1)} %all_to_all.5.parts_ref), custom_call_target="tpu_custom_call" | custom-call | tf_op jit(solution)/shard_map/assemble/pallas_call | solution.py:158
  26.5 0.9 %collective-permute-start.1 = (bf16[64,2048]{1,0:T(8,128)(2,1)}, bf16[64,2048]{1,0:T(8,128)(2,1)S(1)}, u32[]{:S(2)}, u32[]{:S(2)}) collective-permute-start(bf16[64,2048]{1,0:T(8,128)(2,1)} %assemble.1.refs_0_), channel_id=1, source_target_pairs={{0,8},{4,12},{8,0},{12,4},{1,9},{5,13},{9,1},{13,5},{2,10},{6,14},... | collective-permute-start | bytes 786440 | tf_op jit(solution)/shard_map/ppermute | solution.py:290
  27.4 0.0 collective-permute-start
  27.5 1.4 %collective-permute-start.5 = (bf16[64,2048]{1,0:T(8,128)(2,1)}, bf16[64,2048]{1,0:T(8,128)(2,1)S(1)}, u32[]{:S(2)}, u32[]{:S(2)}) collective-permute-start(bf16[64,2048]{1,0:T(8,128)(2,1)} %assemble.1.refs_0_), channel_id=1, source_target_pairs={{0,1},{1,0},{2,3},{3,2},{4,5},{5,4},{6,7},{7,6},{8,9},{9,8},{10,11... | collective-permute-start | bytes 786440 | tf_op jit(solution)/shard_map/ppermute | solution.py:307
  28.9 3.1 %collective-permute-start.2 = (bf16[64,2048]{1,0:T(8,128)(2,1)}, bf16[64,2048]{1,0:T(8,128)(2,1)S(1)}, u32[]{:S(2)}, u32[]{:S(2)}) collective-permute-start(bf16[64,2048]{1,0:T(8,128)(2,1)} %assemble.1.refs_0_), channel_id=1, source_target_pairs={{2,0},{3,1},{6,4},{7,5},{10,8},{11,9},{14,12},{15,13},{18,16},{19,... | collective-permute-start | bytes 786440 | tf_op jit(solution)/shard_map/ppermute | solution.py:303
  32.0 2.9 %collective-permute-done.1.refs_2_ = bf16[64,2048]{1,0:T(8,128)(2,1)S(1)} collective-permute-done((bf16[64,2048]{1,0:T(8,128)(2,1)}, bf16[64,2048]{1,0:T(8,128)(2,1)S(1)}, u32[]{:S(2)}, u32[]{:S(2)}) %collective-permute-start.1) | collective-permute-done | bytes 262176 | tf_op jit(solution)/shard_map/ppermute | solution.py:290
  34.9 1.3 %collective-permute-start.4 = (bf16[64,2048]{1,0:T(8,128)(2,1)S(1)}, bf16[64,2048]{1,0:T(8,128)(2,1)S(1)}, u32[]{:S(2)}, u32[]{:S(2)}) collective-permute-start(bf16[64,2048]{1,0:T(8,128)(2,1)S(1)} %collective-permute-done.1.refs_2_), channel_id=1, source_target_pairs={{0,2},{1,3},{4,6},{5,7},{8,10},{9,11},{12,14},{13,15},{16,18},{17,... | collective-permute-start | bytes 786440 | tf_op jit(solution)/shard_map/ppermute | solution.py:305
  36.2 5.9 %collective-permute-done.refs_1_ = bf16[64,2048]{1,0:T(8,128)(2,1)S(1)} collective-permute-done((bf16[64,2048]{1,0:T(8,128)(2,1)}, bf16[64,2048]{1,0:T(8,128)(2,1)S(1)}, u32[]{:S(2)}, u32[]{:S(2)}) %collective-permute-start) | collective-permute-done | bytes 262176 | tf_op jit(solution)/shard_map/ppermute | solution.py:290
  42.1 1.1 %collective-permute-start.3 = (bf16[64,2048]{1,0:T(8,128)(2,1)S(1)}, bf16[64,2048]{1,0:T(8,128)(2,1)S(1)}, u32[]{:S(2)}, u32[]{:S(2)}) collective-permute-start(bf16[64,2048]{1,0:T(8,128)(2,1)S(1)} %collective-permute-done.refs_1_), channel_id=1, source_target_pairs={{0,2},{2,0},{1,3},{3,1},{4,6},{6,4},{5,7},{7,5},{8,10},{10,8},{9,1... | collective-permute-start | bytes 786440 | tf_op jit(solution)/shard_map/ppermute | solution.py:304
  43.2 0.8 %collective-permute-start.7 = (bf16[64,2048]{1,0:T(8,128)(2,1)S(1)}, bf16[64,2048]{1,0:T(8,128)(2,1)S(1)}, u32[]{:S(2)}, u32[]{:S(2)}) collective-permute-start(bf16[64,2048]{1,0:T(8,128)(2,1)S(1)} %collective-permute-done.1.refs_2_), channel_id=1, source_target_pairs={{0,1},{1,0},{2,3},{3,2},{4,5},{5,4},{6,7},{7,6},{8,9},{9,8},{10,11... | collective-permute-start | bytes 786440 | tf_op jit(solution)/shard_map/ppermute | solution.py:307
  44.0 0.0 collective-permute-done.5.refs_6_
  44.0 0.0 collective-permute-start.6
  44.0 0.0 collective-permute-done.2.refs_3_
  44.0 0.5 collective-permute-start.8
  44.5 0.0 collective-permute-done.4.refs_5_
  44.5 4.2 %collective-permute-start.10 = (bf16[64,2048]{1,0:T(8,128)(2,1)S(1)}, bf16[64,2048]{1,0:T(8,128)(2,1)S(1)}, u32[]{:S(2)}, u32[]{:S(2)}) collective-permute-start(bf16[64,2048]{1,0:T(8,128)(2,1)S(1)} %collective-permute-done.4.refs_5_), channel_id=1, source_target_pairs={{0,1},{1,0},{2,3},{3,2},{4,5},{5,4},{6,7},{7,6},{8,9},{9,8},{10,11... | collective-permute-start | bytes 786440 | tf_op jit(solution)/shard_map/ppermute | solution.py:307
  48.7 1.7 %collective-permute-done.3.refs_4_ = bf16[64,2048]{1,0:T(8,128)(2,1)S(1)} collective-permute-done((bf16[64,2048]{1,0:T(8,128)(2,1)S(1)}, bf16[64,2048]{1,0:T(8,128)(2,1)S(1)}, u32[]{:S(2)}, u32[]{:S(2)}) %collective-permute-start.3) | collective-permute-done | bytes 262176 | tf_op jit(solution)/shard_map/ppermute | solution.py:304
  50.4 2.2 %collective-permute-start.9 = (bf16[64,2048]{1,0:T(8,128)(2,1)S(1)}, bf16[64,2048]{1,0:T(8,128)(2,1)S(1)}, u32[]{:S(2)}, u32[]{:S(2)}) collective-permute-start(bf16[64,2048]{1,0:T(8,128)(2,1)S(1)} %collective-permute-done.3.refs_4_), channel_id=1, source_target_pairs={{0,1},{1,0},{2,3},{3,2},{4,5},{5,4},{6,7},{7,6},{8,9},{9,8},{10,11... | collective-permute-start | bytes 786440 | tf_op jit(solution)/shard_map/ppermute | solution.py:307
  52.5 0.0 collective-permute-done.8.refs_9_
  52.5 0.0 collective-permute-done.7.refs_8_
  52.6 0.0 collective-permute-done.6.refs_7_
  52.6 0.0 collective-permute-done.10.refs_11_
  52.6 1.1 %collective-permute-done.9.refs_10_ = bf16[64,2048]{1,0:T(8,128)(2,1)S(1)} collective-permute-done((bf16[64,2048]{1,0:T(8,128)(2,1)S(1)}, bf16[64,2048]{1,0:T(8,128)(2,1)S(1)}, u32[]{:S(2)}, u32[]{:S(2)}) %collective-permute-start.9) | collective-permute-done | bytes 262176 | tf_op jit(solution)/shard_map/ppermute | solution.py:307
  53.7 0.0 copy-start
  53.7 0.9 %copy-done = bf16[64,2048]{1,0:T(8,128)(2,1)S(1)} copy-done((bf16[64,2048]{1,0:T(8,128)(2,1)S(1)}, bf16[64,2048]{1,0:T(8,128)(2,1)}, u32[]{:S(2)}) %copy-start) | copy-done | bytes 262168
  54.7 15.1 %correlate.1 = bf16[2,32,288,128]{3,2,1,0:T(8,128)(2,1)} custom-call(s32[1]{0:T(128)} %bitcast.core_ref, s32[1]{0:T(128)} %bitcast.1.column_ref, bf16[64,2048]{1,0:T(8,128)(2,1)S(1)} %copy-done, bf16[64,2048]{1,0:T(8,128)(2,1)S(1)} %collective-permute-done.refs_1_, bf16[64,2048]{1,0:T(8,128)(2,1)S(1)} %collective-permute-done.1.refs_2_, ...), custom_call_target="tpu_custom_call" | custom-call | flops 9663676416 | bytes 8388608 | tf_op jit(solution)/shard_map/correlate/pallas_call | solution.py:262
Async XLA Ops:
  26.5 8.4 %collective-permute-start.1 = (bf16[64,2048]{1,0:T(8,128)(2,1)}, bf16[64,2048]{1,0:T(8,128)(2,1)S(1)}, u32[]{:S(2)}, u32[]{:S(2)}) collective-permute-start(bf16[64,2048]{1,0:T(8,128)(2,1)} %assemble.1.refs_0_), channel_id=1, source_target_pairs={{0,8},{4,12},{8,0},{12,4},{1,9},{5,13},{9,1},{13,5},{2,10},{6,14},... | collective-permute-start | bytes 786440 | tf_op jit(solution)/shard_map/ppermute | solution.py:290
  27.4 14.6 %collective-permute-start = (bf16[64,2048]{1,0:T(8,128)(2,1)}, bf16[64,2048]{1,0:T(8,128)(2,1)S(1)}, u32[]{:S(2)}, u32[]{:S(2)}) collective-permute-start(bf16[64,2048]{1,0:T(8,128)(2,1)} %assemble.1.refs_0_), channel_id=1, source_target_pairs={{0,12},{4,0},{8,4},{12,8},{1,13},{5,1},{9,5},{13,9},{2,14},{6,2},{... | collective-permute-start | bytes 786440 | tf_op jit(solution)/shard_map/ppermute | solution.py:290
  27.5 16.5 %collective-permute-start.5 = (bf16[64,2048]{1,0:T(8,128)(2,1)}, bf16[64,2048]{1,0:T(8,128)(2,1)S(1)}, u32[]{:S(2)}, u32[]{:S(2)}) collective-permute-start(bf16[64,2048]{1,0:T(8,128)(2,1)} %assemble.1.refs_0_), channel_id=1, source_target_pairs={{0,1},{1,0},{2,3},{3,2},{4,5},{5,4},{6,7},{7,6},{8,9},{9,8},{10,11... | collective-permute-start | bytes 786440 | tf_op jit(solution)/shard_map/ppermute | solution.py:307
  28.9 15.1 %collective-permute-start.2 = (bf16[64,2048]{1,0:T(8,128)(2,1)}, bf16[64,2048]{1,0:T(8,128)(2,1)S(1)}, u32[]{:S(2)}, u32[]{:S(2)}) collective-permute-start(bf16[64,2048]{1,0:T(8,128)(2,1)} %assemble.1.refs_0_), channel_id=1, source_target_pairs={{2,0},{3,1},{6,4},{7,5},{10,8},{11,9},{14,12},{15,13},{18,16},{19,... | collective-permute-start | bytes 786440 | tf_op jit(solution)/shard_map/ppermute | solution.py:303
  34.9 9.6 %collective-permute-start.4 = (bf16[64,2048]{1,0:T(8,128)(2,1)S(1)}, bf16[64,2048]{1,0:T(8,128)(2,1)S(1)}, u32[]{:S(2)}, u32[]{:S(2)}) collective-permute-start(bf16[64,2048]{1,0:T(8,128)(2,1)S(1)} %collective-permute-done.1.refs_2_), channel_id=1, source_target_pairs={{0,2},{1,3},{4,6},{5,7},{8,10},{9,11},{12,14},{13,15},{16,18},{17,... | collective-permute-start | bytes 786440 | tf_op jit(solution)/shard_map/ppermute | solution.py:305
  42.1 8.3 %collective-permute-start.3 = (bf16[64,2048]{1,0:T(8,128)(2,1)S(1)}, bf16[64,2048]{1,0:T(8,128)(2,1)S(1)}, u32[]{:S(2)}, u32[]{:S(2)}) collective-permute-start(bf16[64,2048]{1,0:T(8,128)(2,1)S(1)} %collective-permute-done.refs_1_), channel_id=1, source_target_pairs={{0,2},{2,0},{1,3},{3,1},{4,6},{6,4},{5,7},{7,5},{8,10},{10,8},{9,1... | collective-permute-start | bytes 786440 | tf_op jit(solution)/shard_map/ppermute | solution.py:304
  43.2 9.3 %collective-permute-start.7 = (bf16[64,2048]{1,0:T(8,128)(2,1)S(1)}, bf16[64,2048]{1,0:T(8,128)(2,1)S(1)}, u32[]{:S(2)}, u32[]{:S(2)}) collective-permute-start(bf16[64,2048]{1,0:T(8,128)(2,1)S(1)} %collective-permute-done.1.refs_2_), channel_id=1, source_target_pairs={{0,1},{1,0},{2,3},{3,2},{4,5},{5,4},{6,7},{7,6},{8,9},{9,8},{10,11... | collective-permute-start | bytes 786440 | tf_op jit(solution)/shard_map/ppermute | solution.py:307
  44.0 8.6 %collective-permute-start.6 = (bf16[64,2048]{1,0:T(8,128)(2,1)S(1)}, bf16[64,2048]{1,0:T(8,128)(2,1)S(1)}, u32[]{:S(2)}, u32[]{:S(2)}) collective-permute-start(bf16[64,2048]{1,0:T(8,128)(2,1)S(1)} %collective-permute-done.refs_1_), channel_id=1, source_target_pairs={{0,1},{1,0},{2,3},{3,2},{4,5},{5,4},{6,7},{7,6},{8,9},{9,8},{10,11... | collective-permute-start | bytes 786440 | tf_op jit(solution)/shard_map/ppermute | solution.py:307
  44.0 8.6 %collective-permute-start.8 = (bf16[64,2048]{1,0:T(8,128)(2,1)S(1)}, bf16[64,2048]{1,0:T(8,128)(2,1)S(1)}, u32[]{:S(2)}, u32[]{:S(2)}) collective-permute-start(bf16[64,2048]{1,0:T(8,128)(2,1)S(1)} %collective-permute-done.2.refs_3_), channel_id=1, source_target_pairs={{0,1},{1,0},{2,3},{3,2},{4,5},{5,4},{6,7},{7,6},{8,9},{9,8},{10,11... | collective-permute-start | bytes 786440 | tf_op jit(solution)/shard_map/ppermute | solution.py:307
  44.5 8.1 %collective-permute-start.10 = (bf16[64,2048]{1,0:T(8,128)(2,1)S(1)}, bf16[64,2048]{1,0:T(8,128)(2,1)S(1)}, u32[]{:S(2)}, u32[]{:S(2)}) collective-permute-start(bf16[64,2048]{1,0:T(8,128)(2,1)S(1)} %collective-permute-done.4.refs_5_), channel_id=1, source_target_pairs={{0,1},{1,0},{2,3},{3,2},{4,5},{5,4},{6,7},{7,6},{8,9},{9,8},{10,11... | collective-permute-start | bytes 786440 | tf_op jit(solution)/shard_map/ppermute | solution.py:307
  50.4 3.3 %collective-permute-start.9 = (bf16[64,2048]{1,0:T(8,128)(2,1)S(1)}, bf16[64,2048]{1,0:T(8,128)(2,1)S(1)}, u32[]{:S(2)}, u32[]{:S(2)}) collective-permute-start(bf16[64,2048]{1,0:T(8,128)(2,1)S(1)} %collective-permute-done.3.refs_4_), channel_id=1, source_target_pairs={{0,1},{1,0},{2,3},{3,2},{4,5},{5,4},{6,7},{7,6},{8,9},{9,8},{10,11... | collective-permute-start | bytes 786440 | tf_op jit(solution)/shard_map/ppermute | solution.py:307
  53.7 0.9 %copy-start = (bf16[64,2048]{1,0:T(8,128)(2,1)S(1)}, bf16[64,2048]{1,0:T(8,128)(2,1)}, u32[]{:S(2)}) copy-start(bf16[64,2048]{1,0:T(8,128)(2,1)} %assemble.1.refs_0_) | copy-start | bytes 786436

commit v4 on v3

--- a/solution.py
+++ b/solution.py
@@ -191,7 +191,7 @@
 def correlate_kernel(core_ref, column_ref, *refs):
     count = HELD
     straight, crossed = refs[:count], refs[count : 2 * count]
-    out_ref, own_ref, span_ref, rows_ref, mine_ref, sems = refs[2 * count :]
+    out_ref, own_ref, span_ref, rows_ref = refs[2 * count :]
     band = pl.program_id(0)
     step = pl.program_id(1)
     row = lax.broadcasted_iota(jnp.int32, (LAGS, LANE), 0)
@@ -199,9 +199,7 @@
     core = core_ref[0]
     column = column_ref[0]
 
-    def gather(blocks, base):
-        first = pltpu.make_async_copy(base, mine_ref, sems.at[0])
-        first.start()
+    def gather(blocks):
         for j in range(1, REACH + 1):
             size = BLOCK if j == REACH else 2 * BLOCK
             start = 2 * BLOCK * j
@@ -220,15 +218,13 @@
                 def _():
                     span_ref[start - BLOCK : start + BLOCK, :] = blocks[source][...]
 
-        first.wait()
-
         @pl.when(core == 0)
         def _():
-            span_ref[: 2 * BLOCK, :] = mine_ref[...]
+            span_ref[: 2 * BLOCK, :] = blocks[0][...]
 
         @pl.when(core == 1)
         def _():
-            span_ref[:BLOCK, :] = mine_ref[BLOCK:, :]
+            span_ref[:BLOCK, :] = blocks[0][BLOCK:, :]
 
         own = span_ref[:BLOCK, :].astype(jnp.float32)
         half = jnp.zeros((BLOCK, LAGS // 2), jnp.float32)
@@ -239,11 +235,11 @@
 
     @pl.when(jnp.logical_and(step == 0, band == 0))
     def _():
-        gather(straight, straight[0])
+        gather(straight)
 
     @pl.when(jnp.logical_and(step == 0, band == 1))
     def _():
-        gather(crossed, crossed[0])
+        gather(crossed)
 
     scale = 1.0 / math.sqrt(TOTAL)
     for pair in range(PAIRS):
@@ -258,13 +254,12 @@
 def correlate(core, column, straight, crossed):
     steps = BLOCK // (2 * PAIRS)
     held = pl.BlockSpec(memory_space=pltpu.VMEM)
-    anywhere = pl.BlockSpec(memory_space=pl.ANY)
     return pl.pallas_call(
         correlate_kernel,
         grid_spec=pltpu.PrefetchScalarGridSpec(
             num_scalar_prefetch=2,
             grid=(2, steps),
-            in_specs=([anywhere] + [held] * (HELD - 1)) * 2,
+            in_specs=[held] * (2 * HELD),
             out_specs=pl.BlockSpec(
                 (1, 2 * PAIRS, SPAN, LAGS), lambda s, c, w, v: (lax.rem(w[0] + s, 2), c, 0, 0)
             ),
@@ -272,8 +267,6 @@
                 pltpu.VMEM((TOTAL // LANE + 1, BLOCK, LANE), jnp.float32),
                 pltpu.VMEM((SPAN, TOTAL), jnp.bfloat16),
                 pltpu.VMEM((2, 2 * LAGS, TOTAL), jnp.bfloat16),
-                pltpu.VMEM((2 * BLOCK, TOTAL), jnp.bfloat16),
-                pltpu.SemaphoreType.DMA((1,)),
             ],
         ),
         out_shape=jax.ShapeDtypeStruct((2, BLOCK, SPAN, LAGS), jnp.bfloat16),
@@ -296,15 +289,17 @@
     parts = lax.all_to_all(parts, ("sub", "core"), split_axis=0, concat_axis=0, tiled=True)
     mine = assemble(parts)
     above, second = up(mine, 1), up(mine, 2)
+    beside = lax.ppermute(mine, "column", [(0, 1), (1, 0)])
     held = [
         mine,
         above,
         second,
-        lax.ppermute(mine, "column", [(1, 0)]),
-        lax.ppermute(above, "column", [(0, 1), (1, 0)]),
+        beside,
+        up(beside, 1),
         lax.ppermute(second, "column", [(0, 1)]),
     ]
     swapped = [lax.ppermute(value, "core", [(0, 1), (1, 0)]) for value in held]
+    held[0] = lax.ppermute(swapped[0], "core", [(0, 1), (1, 0)])
     column = lax.axis_index("column")
     return correlate(core[None], column[None], held, swapped)
 

time: 70 us -> 67.4 us (0.963)
  the two profiles are of different devices: /device:TPU:27 before, /device:TPU:3 now
where the time goes in v4:
time: 67.4 us; the launch traced here: 66.3 us
  Pallas kernels  23.9 us (35%)
  starting transfers between devices  18.4 us (27%)
  blocking collectives  17.6 us (26%)
  waiting for transfers between devices  6.27 us (9%)
    all_to_all x1, blocking collectives, body(): lax.all_to_all(parts, ('sub', 'core'), split_axis=0, concat_axis=0, tiled...  17.6 us
    pallas_call x1, Pallas kernels, correlate(): pl.pallas_call(correlate_kernel, grid_spec=pltpu.PrefetchScalarGridSpec(n...  15 us
    ppermute x6, starting transfers between devices, body(): swapped = [lax.ppermute(value, 'core', [(0, 1), (1, 0)]) for value in held]  9.07 us
    pallas_call x1, Pallas kernels, filter_bank(): pl.pallas_call(filter_kernel, in_specs=[pl.BlockSpec(memory_space=pl.ANY)...  7.19 us
    ppermute x3, starting transfers between devices, up(): return lax.ppermute(value, 'row', pairs)  6.42 us
    ppermute x3, waiting for transfers between devices, up(): return lax.ppermute(value, 'row', pairs)  4.75 us
    pallas_call x1, Pallas kernels, assemble(): pl.pallas_call(assemble_kernel, out_shape=jax.ShapeDtypeStruct((2 * BLOCK...  1.74 us
    ppermute x6, waiting for transfers between devices, body(): swapped = [lax.ppermute(value, 'core', [(0, 1), (1, 0)]) for value in held]  1.52 us
  transfers between devices with their start and end apart: 12, of which 4 were waited for; matrix products, arithmetic and copies ran while one was open for 0% of the time, Pallas kernels for 0%

profile of v4, /device:TPU:3, one launch (start us, length us, event | category | flops | bytes accessed | tf_op | source)
XLA Modules:
  0.0 66.3 jit_solution(14429342355484196437)
XLA Ops:
  0.0 7.2 %filter_bank.1 = bf16[16,32,384]{2,1,0:T(8,128)(2,1)} custom-call(bf16[32,65536]{1,0:T(8,128)(2,1)} %x_hbm.1, s32[1,4096]{1,0:T(1,128)} %bitcast.3, f32[16,256]{1,0:T(8,128)} %constant.10.cos_hbm), custom_call_target="tpu_custom_call" | custom-call | tf_op jit(solution)/shard_map/filter_bank/pallas_call | solution.py:124
  7.2 17.6 %all_to_all.5.parts_ref = bf16[16,32,384]{2,1,0:T(8,128)(2,1)} all-to-all(bf16[16,32,384]{2,1,0:T(8,128)(2,1)} %filter_bank.1), channel_id=1, replica_groups=mesh['sub'=8,'row'=4,'column'=2,'core'=2] {'sub','core'}, dimensions={0} | all-to-all | bytes 786432 | tf_op jit(solution)/shard_map/all_to_all | solution.py:289
  24.8 1.7 %assemble.1 = bf16[64,2048]{1,0:T(8,128)(2,1)} custom-call(bf16[16,32,384]{2,1,0:T(8,128)(2,1)} %all_to_all.5.parts_ref), custom_call_target="tpu_custom_call" | custom-call | tf_op jit(solution)/shard_map/assemble/pallas_call | solution.py:158
  26.5 1.2 %collective-permute-start.4 = (bf16[64,2048]{1,0:T(8,128)(2,1)}, bf16[64,2048]{1,0:T(8,128)(2,1)S(1)}, u32[]{:S(2)}, u32[]{:S(2)}) collective-permute-start(bf16[64,2048]{1,0:T(8,128)(2,1)} %assemble.1), channel_id=1, source_target_pairs={{0,2},{2,0},{1,3},{3,1},{4,6},{6,4},{5,7},{7,5},{8,10},{10,8},{9,1... | collective-permute-start | bytes 786440 | tf_op jit(solution)/shard_map/ppermute | solution.py:292
  27.7 2.9 %collective-permute-start.3 = (bf16[64,2048]{1,0:T(8,128)(2,1)}, bf16[64,2048]{1,0:T(8,128)(2,1)S(1)}, u32[]{:S(2)}, u32[]{:S(2)}) collective-permute-start(bf16[64,2048]{1,0:T(8,128)(2,1)} %assemble.1), channel_id=1, source_target_pairs={{0,8},{4,12},{8,0},{12,4},{1,9},{5,13},{9,1},{13,5},{2,10},{6,14},... | collective-permute-start | bytes 786440 | tf_op jit(solution)/shard_map/ppermute | solution.py:283
  30.6 0.8 %collective-permute-start.2 = (bf16[64,2048]{1,0:T(8,128)(2,1)}, bf16[64,2048]{1,0:T(8,128)(2,1)S(1)}, u32[]{:S(2)}, u32[]{:S(2)}) collective-permute-start(bf16[64,2048]{1,0:T(8,128)(2,1)} %assemble.1), channel_id=1, source_target_pairs={{0,12},{4,0},{8,4},{12,8},{1,13},{5,1},{9,5},{13,9},{2,14},{6,2},{... | collective-permute-start | bytes 786440 | tf_op jit(solution)/shard_map/ppermute | solution.py:283
  31.3 2.0 %collective-permute-start = (bf16[64,2048]{1,0:T(8,128)(2,1)}, bf16[64,2048]{1,0:T(8,128)(2,1)S(1)}, u32[]{:S(2)}, u32[]{:S(2)}) collective-permute-start(bf16[64,2048]{1,0:T(8,128)(2,1)} %assemble.1), channel_id=1, source_target_pairs={{0,1},{1,0},{2,3},{3,2},{4,5},{5,4},{6,7},{7,6},{8,9},{9,8},{10,11... | collective-permute-start | bytes 786440 | tf_op jit(solution)/shard_map/ppermute | solution.py:301
  33.3 0.0 collective-permute-done.4.refs_3_
  33.3 2.1 %collective-permute-start.9 = (bf16[64,2048]{1,0:T(8,128)(2,1)S(1)}, bf16[64,2048]{1,0:T(8,128)(2,1)S(1)}, u32[]{:S(2)}, u32[]{:S(2)}) collective-permute-start(bf16[64,2048]{1,0:T(8,128)(2,1)S(1)} %collective-permute-done.4.refs_3_), channel_id=1, source_target_pairs={{0,1},{1,0},{2,3},{3,2},{4,5},{5,4},{6,7},{7,6},{8,9},{9,8},{10,11... | collective-permute-start | bytes 786440 | tf_op jit(solution)/shard_map/ppermute | solution.py:301
  35.4 2.7 %collective-permute-start.5 = (bf16[64,2048]{1,0:T(8,128)(2,1)S(1)}, bf16[64,2048]{1,0:T(8,128)(2,1)S(1)}, u32[]{:S(2)}, u32[]{:S(2)}) collective-permute-start(bf16[64,2048]{1,0:T(8,128)(2,1)S(1)} %collective-permute-done.4.refs_3_), channel_id=1, source_target_pairs={{0,12},{4,0},{8,4},{12,8},{1,13},{5,1},{9,5},{13,9},{2,14},{6,2},{... | collective-permute-start | bytes 786440 | tf_op jit(solution)/shard_map/ppermute | solution.py:283
  38.2 0.0 collective-permute-done.3.refs_2_
  38.2 1.3 %collective-permute-start.6 = (bf16[64,2048]{1,0:T(8,128)(2,1)S(1)}, bf16[64,2048]{1,0:T(8,128)(2,1)S(1)}, u32[]{:S(2)}, u32[]{:S(2)}) collective-permute-start(bf16[64,2048]{1,0:T(8,128)(2,1)S(1)} %collective-permute-done.3.refs_2_), channel_id=1, source_target_pairs={{0,2},{1,3},{4,6},{5,7},{8,10},{9,11},{12,14},{13,15},{16,18},{17,... | collective-permute-start | bytes 786440 | tf_op jit(solution)/shard_map/ppermute | solution.py:299
  39.5 3.2 %collective-permute-done.2.refs_1_ = bf16[64,2048]{1,0:T(8,128)(2,1)S(1)} collective-permute-done((bf16[64,2048]{1,0:T(8,128)(2,1)}, bf16[64,2048]{1,0:T(8,128)(2,1)S(1)}, u32[]{:S(2)}, u32[]{:S(2)}) %collective-permute-start.2) | collective-permute-done | bytes 262176 | tf_op jit(solution)/shard_map/ppermute | solution.py:283
  42.6 3.4 %collective-permute-start.8 = (bf16[64,2048]{1,0:T(8,128)(2,1)S(1)}, bf16[64,2048]{1,0:T(8,128)(2,1)S(1)}, u32[]{:S(2)}, u32[]{:S(2)}) collective-permute-start(bf16[64,2048]{1,0:T(8,128)(2,1)S(1)} %collective-permute-done.3.refs_2_), channel_id=1, source_target_pairs={{0,1},{1,0},{2,3},{3,2},{4,5},{5,4},{6,7},{7,6},{8,9},{9,8},{10,11... | collective-permute-start | bytes 786440 | tf_op jit(solution)/shard_map/ppermute | solution.py:301
  46.1 0.0 collective-permute-done.refs_6_
  46.1 0.0 collective-permute-start.7
  46.1 0.0 collective-permute-done.9.refs_9_
  46.1 0.5 collective-permute-start.1
  46.6 1.6 %collective-permute-done.5.refs_4_ = bf16[64,2048]{1,0:T(8,128)(2,1)S(1)} collective-permute-done((bf16[64,2048]{1,0:T(8,128)(2,1)S(1)}, bf16[64,2048]{1,0:T(8,128)(2,1)S(1)}, u32[]{:S(2)}, u32[]{:S(2)}) %collective-permute-start.5) | collective-permute-done | bytes 262176 | tf_op jit(solution)/shard_map/ppermute | solution.py:283
  48.1 1.6 %collective-permute-start.10 = (bf16[64,2048]{1,0:T(8,128)(2,1)S(1)}, bf16[64,2048]{1,0:T(8,128)(2,1)S(1)}, u32[]{:S(2)}, u32[]{:S(2)}) collective-permute-start(bf16[64,2048]{1,0:T(8,128)(2,1)S(1)} %collective-permute-done.5.refs_4_), channel_id=1, source_target_pairs={{0,1},{1,0},{2,3},{3,2},{4,5},{5,4},{6,7},{7,6},{8,9},{9,8},{10,11... | collective-permute-start | bytes 786440 | tf_op jit(solution)/shard_map/ppermute | solution.py:301
  49.7 0.0 collective-permute-done.6.refs_5_
  49.7 0.0 collective-permute-start.11
  49.7 0.0 collective-permute-done.8.refs_8_
  49.7 0.0 collective-permute-done.7.refs_7_
  49.7 0.0 collective-permute-done.1.refs_0_
  49.7 1.1 %collective-permute-done.10.refs_10_ = bf16[64,2048]{1,0:T(8,128)(2,1)S(1)} collective-permute-done((bf16[64,2048]{1,0:T(8,128)(2,1)S(1)}, bf16[64,2048]{1,0:T(8,128)(2,1)S(1)}, u32[]{:S(2)}, u32[]{:S(2)}) %collective-permute-start.10) | collective-permute-done | bytes 262176 | tf_op jit(solution)/shard_map/ppermute | solution.py:301
  50.9 0.4 collective-permute-done.11.refs_11_
  51.2 15.0 %correlate.1 = bf16[2,32,288,128]{3,2,1,0:T(8,128)(2,1)} custom-call(s32[1]{0:T(128)} %bitcast.core_ref, s32[1]{0:T(128)} %bitcast.1.column_ref, bf16[64,2048]{1,0:T(8,128)(2,1)S(1)} %collective-permute-done.1.refs_0_, bf16[64,2048]{1,0:T(8,128)(2,1)S(1)} %collective-permute-done.2.refs_1_, bf16[64,2048]{1,0:T(8,128)(2,1)S(1)} %collective-permute-done.3.refs_2_, ...), custom_call_target="tpu_custom_call" | custom-call | flops 9663676416 | bytes 8388608 | tf_op jit(solution)/shard_map/correlate/pallas_call | solution.py:257
Async XLA Ops:
  26.5 6.8 %collective-permute-start.4 = (bf16[64,2048]{1,0:T(8,128)(2,1)}, bf16[64,2048]{1,0:T(8,128)(2,1)S(1)}, u32[]{:S(2)}, u32[]{:S(2)}) collective-permute-start(bf16[64,2048]{1,0:T(8,128)(2,1)} %assemble.1), channel_id=1, source_target_pairs={{0,2},{2,0},{1,3},{3,1},{4,6},{6,4},{5,7},{7,5},{8,10},{10,8},{9,1... | collective-permute-start | bytes 786440 | tf_op jit(solution)/shard_map/ppermute | solution.py:292
  27.7 10.5 %collective-permute-start.3 = (bf16[64,2048]{1,0:T(8,128)(2,1)}, bf16[64,2048]{1,0:T(8,128)(2,1)S(1)}, u32[]{:S(2)}, u32[]{:S(2)}) collective-permute-start(bf16[64,2048]{1,0:T(8,128)(2,1)} %assemble.1), channel_id=1, source_target_pairs={{0,8},{4,12},{8,0},{12,4},{1,9},{5,13},{9,1},{13,5},{2,10},{6,14},... | collective-permute-start | bytes 786440 | tf_op jit(solution)/shard_map/ppermute | solution.py:283
  30.6 12.1 %collective-permute-start.2 = (bf16[64,2048]{1,0:T(8,128)(2,1)}, bf16[64,2048]{1,0:T(8,128)(2,1)S(1)}, u32[]{:S(2)}, u32[]{:S(2)}) collective-permute-start(bf16[64,2048]{1,0:T(8,128)(2,1)} %assemble.1), channel_id=1, source_target_pairs={{0,12},{4,0},{8,4},{12,8},{1,13},{5,1},{9,5},{13,9},{2,14},{6,2},{... | collective-permute-start | bytes 786440 | tf_op jit(solution)/shard_map/ppermute | solution.py:283
  31.3 14.7 %collective-permute-start = (bf16[64,2048]{1,0:T(8,128)(2,1)}, bf16[64,2048]{1,0:T(8,128)(2,1)S(1)}, u32[]{:S(2)}, u32[]{:S(2)}) collective-permute-start(bf16[64,2048]{1,0:T(8,128)(2,1)} %assemble.1), channel_id=1, source_target_pairs={{0,1},{1,0},{2,3},{3,2},{4,5},{5,4},{6,7},{7,6},{8,9},{9,8},{10,11... | collective-permute-start | bytes 786440 | tf_op jit(solution)/shard_map/ppermute | solution.py:301
  33.3 12.7 %collective-permute-start.9 = (bf16[64,2048]{1,0:T(8,128)(2,1)S(1)}, bf16[64,2048]{1,0:T(8,128)(2,1)S(1)}, u32[]{:S(2)}, u32[]{:S(2)}) collective-permute-start(bf16[64,2048]{1,0:T(8,128)(2,1)S(1)} %collective-permute-done.4.refs_3_), channel_id=1, source_target_pairs={{0,1},{1,0},{2,3},{3,2},{4,5},{5,4},{6,7},{7,6},{8,9},{9,8},{10,11... | collective-permute-start | bytes 786440 | tf_op jit(solution)/shard_map/ppermute | solution.py:301
  35.4 12.7 %collective-permute-start.5 = (bf16[64,2048]{1,0:T(8,128)(2,1)S(1)}, bf16[64,2048]{1,0:T(8,128)(2,1)S(1)}, u32[]{:S(2)}, u32[]{:S(2)}) collective-permute-start(bf16[64,2048]{1,0:T(8,128)(2,1)S(1)} %collective-permute-done.4.refs_3_), channel_id=1, source_target_pairs={{0,12},{4,0},{8,4},{12,8},{1,13},{5,1},{9,5},{13,9},{2,14},{6,2},{... | collective-permute-start | bytes 786440 | tf_op jit(solution)/shard_map/ppermute | solution.py:283
  38.2 11.5 %collective-permute-start.6 = (bf16[64,2048]{1,0:T(8,128)(2,1)S(1)}, bf16[64,2048]{1,0:T(8,128)(2,1)S(1)}, u32[]{:S(2)}, u32[]{:S(2)}) collective-permute-start(bf16[64,2048]{1,0:T(8,128)(2,1)S(1)} %collective-permute-done.3.refs_2_), channel_id=1, source_target_pairs={{0,2},{1,3},{4,6},{5,7},{8,10},{9,11},{12,14},{13,15},{16,18},{17,... | collective-permute-start | bytes 786440 | tf_op jit(solution)/shard_map/ppermute | solution.py:299
  42.6 7.1 %collective-permute-start.8 = (bf16[64,2048]{1,0:T(8,128)(2,1)S(1)}, bf16[64,2048]{1,0:T(8,128)(2,1)S(1)}, u32[]{:S(2)}, u32[]{:S(2)}) collective-permute-start(bf16[64,2048]{1,0:T(8,128)(2,1)S(1)} %collective-permute-done.3.refs_2_), channel_id=1, source_target_pairs={{0,1},{1,0},{2,3},{3,2},{4,5},{5,4},{6,7},{7,6},{8,9},{9,8},{10,11... | collective-permute-start | bytes 786440 | tf_op jit(solution)/shard_map/ppermute | solution.py:301
  46.1 3.7 %collective-permute-start.7 = (bf16[64,2048]{1,0:T(8,128)(2,1)S(1)}, bf16[64,2048]{1,0:T(8,128)(2,1)S(1)}, u32[]{:S(2)}, u32[]{:S(2)}) collective-permute-start(bf16[64,2048]{1,0:T(8,128)(2,1)S(1)} %collective-permute-done.2.refs_1_), channel_id=1, source_target_pairs={{0,1},{1,0},{2,3},{3,2},{4,5},{5,4},{6,7},{7,6},{8,9},{9,8},{10,11... | collective-permute-start | bytes 786440 | tf_op jit(solution)/shard_map/ppermute | solution.py:301
  46.1 3.7 %collective-permute-start.1 = (bf16[64,2048]{1,0:T(8,128)(2,1)S(1)}, bf16[64,2048]{1,0:T(8,128)(2,1)S(1)}, u32[]{:S(2)}, u32[]{:S(2)}) collective-permute-start(bf16[64,2048]{1,0:T(8,128)(2,1)S(1)} %collective-permute-done.refs_6_), channel_id=1, source_target_pairs={{0,1},{1,0},{2,3},{3,2},{4,5},{5,4},{6,7},{7,6},{8,9},{9,8},{10,11... | collective-permute-start | bytes 786440 | tf_op jit(solution)/shard_map/ppermute | solution.py:302
  48.1 2.7 %collective-permute-start.10 = (bf16[64,2048]{1,0:T(8,128)(2,1)S(1)}, bf16[64,2048]{1,0:T(8,128)(2,1)S(1)}, u32[]{:S(2)}, u32[]{:S(2)}) collective-permute-start(bf16[64,2048]{1,0:T(8,128)(2,1)S(1)} %collective-permute-done.5.refs_4_), channel_id=1, source_target_pairs={{0,1},{1,0},{2,3},{3,2},{4,5},{5,4},{6,7},{7,6},{8,9},{9,8},{10,11... | collective-permute-start | bytes 786440 | tf_op jit(solution)/shard_map/ppermute | solution.py:301
  49.7 1.5 %collective-permute-start.11 = (bf16[64,2048]{1,0:T(8,128)(2,1)S(1)}, bf16[64,2048]{1,0:T(8,128)(2,1)S(1)}, u32[]{:S(2)}, u32[]{:S(2)}) collective-permute-start(bf16[64,2048]{1,0:T(8,128)(2,1)S(1)} %collective-permute-done.6.refs_5_), channel_id=1, source_target_pairs={{0,1},{1,0},{2,3},{3,2},{4,5},{5,4},{6,7},{7,6},{8,9},{9,8},{10,11... | collective-permute-start | bytes 786440 | tf_op jit(solution)/shard_map/ppermute | solution.py:301

commit v5 on v4

--- a/solution.py
+++ b/solution.py
@@ -141,14 +141,14 @@
 
 
 def assemble_kernel(parts_ref, out_ref):
-    for core in range(2):
-        rows = slice(core * BLOCK, (core + 1) * BLOCK)
+    for band in range(2):
+        rows = slice(band * BLOCK, (band + 1) * BLOCK)
         for block in range(N_SUB):
-            here = parts_ref[block * 2 + core]
+            here = parts_ref[block * 2 + band]
             start = block * T_DEV
             head = here[:, :LANE]
             if block:
-                tail = parts_ref[(block - 1) * 2 + core][:, T_DEV:]
+                tail = parts_ref[(block - 1) * 2 + band][:, T_DEV:]
                 head = (head.astype(jnp.float32) + tail.astype(jnp.float32)).astype(jnp.bfloat16)
             out_ref[rows, start : start + LANE] = head
             out_ref[rows, start + LANE : start + T_DEV] = here[:, LANE:T_DEV]
@@ -185,7 +185,7 @@
 
 
 def chip_source(j, column):
-    return {1: (3, 4), 2: (1, 1), 3: (4, 5), 4: (2, 2)}[j][column]
+    return {0: (0, 0), 1: (3, 4), 2: (1, 1), 3: (4, 5), 4: (2, 2)}[j][column]
 
 
 def correlate_kernel(core_ref, column_ref, *refs):
@@ -199,32 +199,27 @@
     core = core_ref[0]
     column = column_ref[0]
 
-    def gather(blocks):
-        for j in range(1, REACH + 1):
-            size = BLOCK if j == REACH else 2 * BLOCK
-            start = 2 * BLOCK * j
-
-            columns = {}
+    def gather(s):
+        part = slice(s * BLOCK, (s + 1) * BLOCK)
+        for k in range(SPAN // BLOCK):
+            place = slice(k * BLOCK, (k + 1) * BLOCK)
+            arrays = crossed if k % 2 else straight
+            cases = {}
             for number in range(2):
-                columns.setdefault(chip_source(j, number), []).append(number)
-            for source, which in columns.items():
-                here = (column >= which[0]) & (column <= which[-1])
-
-                @pl.when(here & (core == 0))
+                for half in range(2):
+                    j = (half + k) // 2
+                    cases.setdefault(chip_source(j, number), []).append((number, half))
+            for source, which in cases.items():
+                if len(which) == 4:
+                    span_ref[place, :] = arrays[source][part, :]
+                    continue
+                here = functools.reduce(
+                    jnp.logical_or, [(column == number) & (core == half) for number, half in which]
+                )
+
+                @pl.when(here)
                 def _():
-                    span_ref[start : start + size, :] = blocks[source][:size, :]
-
-                @pl.when(here & (core == 1))
-                def _():
-                    span_ref[start - BLOCK : start + BLOCK, :] = blocks[source][...]
-
-        @pl.when(core == 0)
-        def _():
-            span_ref[: 2 * BLOCK, :] = blocks[0][...]
-
-        @pl.when(core == 1)
-        def _():
-            span_ref[:BLOCK, :] = blocks[0][BLOCK:, :]
+                    span_ref[place, :] = arrays[source][part, :]
 
         own = span_ref[:BLOCK, :].astype(jnp.float32)
         half = jnp.zeros((BLOCK, LAGS // 2), jnp.float32)
@@ -235,11 +230,11 @@
 
     @pl.when(jnp.logical_and(step == 0, band == 0))
     def _():
-        gather(straight)
+        gather(0)
 
     @pl.when(jnp.logical_and(step == 0, band == 1))
     def _():
-        gather(crossed)
+        gather(1)
 
     scale = 1.0 / math.sqrt(TOTAL)
     for pair in range(PAIRS):
@@ -261,7 +256,7 @@
             grid=(2, steps),
             in_specs=[held] * (2 * HELD),
             out_specs=pl.BlockSpec(
-                (1, 2 * PAIRS, SPAN, LAGS), lambda s, c, w, v: (lax.rem(w[0] + s, 2), c, 0, 0)
+                (1, 2 * PAIRS, SPAN, LAGS), lambda s, c, w, v: (s, c, 0, 0)
             ),
             scratch_shapes=[
                 pltpu.VMEM((TOTAL // LANE + 1, BLOCK, LANE), jnp.float32),
@@ -286,7 +281,7 @@
 def body(samples, taps):
     core = lax.axis_index("core")
     parts = filter_bank(samples, taps[None], cosine_matrix())
-    parts = lax.all_to_all(parts, ("sub", "core"), split_axis=0, concat_axis=0, tiled=True)
+    parts = lax.all_to_all(parts, "sub", split_axis=0, concat_axis=0, tiled=True)
     mine = assemble(parts)
     above, second = up(mine, 1), up(mine, 2)
     beside = lax.ppermute(mine, "column", [(0, 1), (1, 0)])

time: 67.4 us -> 65.2 us (0.967)
  starting transfers between devices: 18.4 us -> 21.2 us
  waiting for transfers between devices: 6.27 us -> 3.47 us
  blocking collectives: 17.6 us -> 15.3 us
    ppermute x3, waiting for transfers between devices: 4.75 us -> 1.95 us  [up(): return lax.ppermute(value, 'row', pairs)]
    ppermute x6, starting transfers between devices: 9.07 us -> 11.9 us  [body(): swapped = [lax.ppermute(value, 'core', [(0, 1), (1, 0)]) for value in held]]
    all_to_all x1, blocking collectives: 17.6 us -> 15.3 us  [body(): lax.all_to_all(parts, 'sub', split_axis=0, concat_axis=0, tiled=True)]
  transfers between devices with their start and end apart: 12 -> 12, of which waited for: 4 -> 3; matrix products, arithmetic and copies ran while one was open for 0% -> 0% of each run, Pallas kernels for 0% -> 0%
where the time goes in v5:
time: 65.2 us; the launch traced here: 64 us
  Pallas kernels  23.9 us (37%)
  starting transfers between devices  21.2 us (33%)
  blocking collectives  15.3 us (23%)
  waiting for transfers between devices  3.47 us (5%)
    all_to_all x1, blocking collectives, body(): lax.all_to_all(parts, 'sub', split_axis=0, concat_axis=0, tiled=True)  15.3 us
    pallas_call x1, Pallas kernels, correlate(): pl.pallas_call(correlate_kernel, grid_spec=pltpu.PrefetchScalarGridSpec(n...  15 us
    ppermute x6, starting transfers between devices, body(): swapped = [lax.ppermute(value, 'core', [(0, 1), (1, 0)]) for value in held]  11.9 us
    pallas_call x1, Pallas kernels, filter_bank(): pl.pallas_call(filter_kernel, in_specs=[pl.BlockSpec(memory_space=pl.ANY)...  7.19 us
    ppermute x3, starting transfers between devices, up(): return lax.ppermute(value, 'row', pairs)  6.45 us
    ppermute x3, waiting for transfers between devices, up(): return lax.ppermute(value, 'row', pairs)  1.95 us
    pallas_call x1, Pallas kernels, assemble(): pl.pallas_call(assemble_kernel, out_shape=jax.ShapeDtypeStruct((2 * BLOCK...  1.74 us
    ppermute x6, waiting for transfers between devices, body(): swapped = [lax.ppermute(value, 'core', [(0, 1), (1, 0)]) for value in held]  1.52 us
  transfers between devices with their start and end apart: 12, of which 3 were waited for; matrix products, arithmetic and copies ran while one was open for 0% of the time, Pallas kernels for 0%

profile of v5, /device:TPU:3, one launch (start us, length us, event | category | flops | bytes accessed | tf_op | source)
XLA Modules:
  0.0 64.0 jit_solution(15692984931219600359)
XLA Ops:
  0.0 7.2 %filter_bank.1 = bf16[16,32,384]{2,1,0:T(8,128)(2,1)} custom-call(bf16[32,65536]{1,0:T(8,128)(2,1)} %x_hbm.1, s32[1,4096]{1,0:T(1,128)} %bitcast.3, f32[16,256]{1,0:T(8,128)} %constant.10.cos_hbm), custom_call_target="tpu_custom_call" | custom-call | tf_op jit(solution)/shard_map/filter_bank/pallas_call | solution.py:124
  7.2 15.3 %all_to_all.5.parts_ref = bf16[16,32,384]{2,1,0:T(8,128)(2,1)} all-to-all(bf16[16,32,384]{2,1,0:T(8,128)(2,1)} %filter_bank.1), channel_id=1, replica_groups=mesh['sub'=8,'row'=4,'column'=2,'core'=2] {'sub'}, dimensions={0} | all-to-all | bytes 786432 | tf_op jit(solution)/shard_map/all_to_all | solution.py:284
  22.5 1.7 %assemble.1 = bf16[64,2048]{1,0:T(8,128)(2,1)} custom-call(bf16[16,32,384]{2,1,0:T(8,128)(2,1)} %all_to_all.5.parts_ref), custom_call_target="tpu_custom_call" | custom-call | tf_op jit(solution)/shard_map/assemble/pallas_call | solution.py:158
  24.3 1.1 %collective-permute-start.4 = (bf16[64,2048]{1,0:T(8,128)(2,1)}, bf16[64,2048]{1,0:T(8,128)(2,1)S(1)}, u32[]{:S(2)}, u32[]{:S(2)}) collective-permute-start(bf16[64,2048]{1,0:T(8,128)(2,1)} %assemble.1), channel_id=1, source_target_pairs={{0,2},{2,0},{1,3},{3,1},{4,6},{6,4},{5,7},{7,5},{8,10},{10,8},{9,1... | collective-permute-start | bytes 786440 | tf_op jit(solution)/shard_map/ppermute | solution.py:287
  25.4 2.9 %collective-permute-start.3 = (bf16[64,2048]{1,0:T(8,128)(2,1)}, bf16[64,2048]{1,0:T(8,128)(2,1)S(1)}, u32[]{:S(2)}, u32[]{:S(2)}) collective-permute-start(bf16[64,2048]{1,0:T(8,128)(2,1)} %assemble.1), channel_id=1, source_target_pairs={{0,8},{4,12},{8,0},{12,4},{1,9},{5,13},{9,1},{13,5},{2,10},{6,14},... | collective-permute-start | bytes 786440 | tf_op jit(solution)/shard_map/ppermute | solution.py:278
  28.3 0.8 %collective-permute-start.2 = (bf16[64,2048]{1,0:T(8,128)(2,1)}, bf16[64,2048]{1,0:T(8,128)(2,1)S(1)}, u32[]{:S(2)}, u32[]{:S(2)}) collective-permute-start(bf16[64,2048]{1,0:T(8,128)(2,1)} %assemble.1), channel_id=1, source_target_pairs={{0,12},{4,0},{8,4},{12,8},{1,13},{5,1},{9,5},{13,9},{2,14},{6,2},{... | collective-permute-start | bytes 786440 | tf_op jit(solution)/shard_map/ppermute | solution.py:278
  29.1 3.4 %collective-permute-start = (bf16[64,2048]{1,0:T(8,128)(2,1)}, bf16[64,2048]{1,0:T(8,128)(2,1)S(1)}, u32[]{:S(2)}, u32[]{:S(2)}) collective-permute-start(bf16[64,2048]{1,0:T(8,128)(2,1)} %assemble.1), channel_id=1, source_target_pairs={{0,1},{1,0},{2,3},{3,2},{4,5},{5,4},{6,7},{7,6},{8,9},{9,8},{10,11... | collective-permute-start | bytes 786440 | tf_op jit(solution)/shard_map/ppermute | solution.py:296
  32.5 0.0 collective-permute-done.4.refs_3_
  32.5 0.9 %collective-permute-start.9 = (bf16[64,2048]{1,0:T(8,128)(2,1)S(1)}, bf16[64,2048]{1,0:T(8,128)(2,1)S(1)}, u32[]{:S(2)}, u32[]{:S(2)}) collective-permute-start(bf16[64,2048]{1,0:T(8,128)(2,1)S(1)} %collective-permute-done.4.refs_3_), channel_id=1, source_target_pairs={{0,1},{1,0},{2,3},{3,2},{4,5},{5,4},{6,7},{7,6},{8,9},{9,8},{10,11... | collective-permute-start | bytes 786440 | tf_op jit(solution)/shard_map/ppermute | solution.py:296
  33.4 2.7 %collective-permute-start.5 = (bf16[64,2048]{1,0:T(8,128)(2,1)S(1)}, bf16[64,2048]{1,0:T(8,128)(2,1)S(1)}, u32[]{:S(2)}, u32[]{:S(2)}) collective-permute-start(bf16[64,2048]{1,0:T(8,128)(2,1)S(1)} %collective-permute-done.4.refs_3_), channel_id=1, source_target_pairs={{0,12},{4,0},{8,4},{12,8},{1,13},{5,1},{9,5},{13,9},{2,14},{6,2},{... | collective-permute-start | bytes 786440 | tf_op jit(solution)/shard_map/ppermute | solution.py:278
  36.1 0.0 collective-permute-done.3.refs_2_
  36.1 1.3 %collective-permute-start.6 = (bf16[64,2048]{1,0:T(8,128)(2,1)S(1)}, bf16[64,2048]{1,0:T(8,128)(2,1)S(1)}, u32[]{:S(2)}, u32[]{:S(2)}) collective-permute-start(bf16[64,2048]{1,0:T(8,128)(2,1)S(1)} %collective-permute-done.3.refs_2_), channel_id=1, source_target_pairs={{0,2},{1,3},{4,6},{5,7},{8,10},{9,11},{12,14},{13,15},{16,18},{17,... | collective-permute-start | bytes 786440 | tf_op jit(solution)/shard_map/ppermute | solution.py:294
  37.4 1.9 %collective-permute-done.2.refs_1_ = bf16[64,2048]{1,0:T(8,128)(2,1)S(1)} collective-permute-done((bf16[64,2048]{1,0:T(8,128)(2,1)}, bf16[64,2048]{1,0:T(8,128)(2,1)S(1)}, u32[]{:S(2)}, u32[]{:S(2)}) %collective-permute-start.2) | collective-permute-done | bytes 262176 | tf_op jit(solution)/shard_map/ppermute | solution.py:278
  39.3 5.3 %collective-permute-start.8 = (bf16[64,2048]{1,0:T(8,128)(2,1)S(1)}, bf16[64,2048]{1,0:T(8,128)(2,1)S(1)}, u32[]{:S(2)}, u32[]{:S(2)}) collective-permute-start(bf16[64,2048]{1,0:T(8,128)(2,1)S(1)} %collective-permute-done.3.refs_2_), channel_id=1, source_target_pairs={{0,1},{1,0},{2,3},{3,2},{4,5},{5,4},{6,7},{7,6},{8,9},{9,8},{10,11... | collective-permute-start | bytes 786440 | tf_op jit(solution)/shard_map/ppermute | solution.py:296
  44.7 0.0 collective-permute-done.refs_6_
  44.7 0.0 collective-permute-start.7
  44.7 0.0 collective-permute-done.9.refs_9_
  44.7 0.5 collective-permute-start.1
  45.2 0.0 collective-permute-done.5.refs_4_
  45.2 2.3 %collective-permute-start.10 = (bf16[64,2048]{1,0:T(8,128)(2,1)S(1)}, bf16[64,2048]{1,0:T(8,128)(2,1)S(1)}, u32[]{:S(2)}, u32[]{:S(2)}) collective-permute-start(bf16[64,2048]{1,0:T(8,128)(2,1)S(1)} %collective-permute-done.5.refs_4_), channel_id=1, source_target_pairs={{0,1},{1,0},{2,3},{3,2},{4,5},{5,4},{6,7},{7,6},{8,9},{9,8},{10,11... | collective-permute-start | bytes 786440 | tf_op jit(solution)/shard_map/ppermute | solution.py:296
  47.5 0.0 collective-permute-done.6.refs_5_
  47.5 0.0 collective-permute-start.11
  47.5 0.0 collective-permute-done.8.refs_8_
  47.5 0.0 collective-permute-done.7.refs_7_
  47.5 0.0 collective-permute-done.1.refs_0_
  47.5 1.1 %collective-permute-done.10.refs_10_ = bf16[64,2048]{1,0:T(8,128)(2,1)S(1)} collective-permute-done((bf16[64,2048]{1,0:T(8,128)(2,1)S(1)}, bf16[64,2048]{1,0:T(8,128)(2,1)S(1)}, u32[]{:S(2)}, u32[]{:S(2)}) %collective-permute-start.10) | collective-permute-done | bytes 262176 | tf_op jit(solution)/shard_map/ppermute | solution.py:296
  48.6 0.4 collective-permute-done.11.refs_11_
  49.0 15.0 %correlate.1 = bf16[2,32,288,128]{3,2,1,0:T(8,128)(2,1)} custom-call(s32[1]{0:T(128)} %bitcast.core_ref, s32[1]{0:T(128)} %bitcast.1.column_ref, bf16[64,2048]{1,0:T(8,128)(2,1)S(1)} %collective-permute-done.1.refs_0_, bf16[64,2048]{1,0:T(8,128)(2,1)S(1)} %collective-permute-done.2.refs_1_, bf16[64,2048]{1,0:T(8,128)(2,1)S(1)} %collective-permute-done.3.refs_2_, ...), custom_call_target="tpu_custom_call" | custom-call | flops 9663676416 | bytes 8388608 | tf_op jit(solution)/shard_map/correlate/pallas_call | solution.py:252
Async XLA Ops:
  24.3 8.2 %collective-permute-start.4 = (bf16[64,2048]{1,0:T(8,128)(2,1)}, bf16[64,2048]{1,0:T(8,128)(2,1)S(1)}, u32[]{:S(2)}, u32[]{:S(2)}) collective-permute-start(bf16[64,2048]{1,0:T(8,128)(2,1)} %assemble.1), channel_id=1, source_target_pairs={{0,2},{2,0},{1,3},{3,1},{4,6},{6,4},{5,7},{7,5},{8,10},{10,8},{9,1... | collective-permute-start | bytes 786440 | tf_op jit(solution)/shard_map/ppermute | solution.py:287
  25.4 10.7 %collective-permute-start.3 = (bf16[64,2048]{1,0:T(8,128)(2,1)}, bf16[64,2048]{1,0:T(8,128)(2,1)S(1)}, u32[]{:S(2)}, u32[]{:S(2)}) collective-permute-start(bf16[64,2048]{1,0:T(8,128)(2,1)} %assemble.1), channel_id=1, source_target_pairs={{0,8},{4,12},{8,0},{12,4},{1,9},{5,13},{9,1},{13,5},{2,10},{6,14},... | collective-permute-start | bytes 786440 | tf_op jit(solution)/shard_map/ppermute | solution.py:278
  28.3 11.0 %collective-permute-start.2 = (bf16[64,2048]{1,0:T(8,128)(2,1)}, bf16[64,2048]{1,0:T(8,128)(2,1)S(1)}, u32[]{:S(2)}, u32[]{:S(2)}) collective-permute-start(bf16[64,2048]{1,0:T(8,128)(2,1)} %assemble.1), channel_id=1, source_target_pairs={{0,12},{4,0},{8,4},{12,8},{1,13},{5,1},{9,5},{13,9},{2,14},{6,2},{... | collective-permute-start | bytes 786440 | tf_op jit(solution)/shard_map/ppermute | solution.py:278
  29.1 15.6 %collective-permute-start = (bf16[64,2048]{1,0:T(8,128)(2,1)}, bf16[64,2048]{1,0:T(8,128)(2,1)S(1)}, u32[]{:S(2)}, u32[]{:S(2)}) collective-permute-start(bf16[64,2048]{1,0:T(8,128)(2,1)} %assemble.1), channel_id=1, source_target_pairs={{0,1},{1,0},{2,3},{3,2},{4,5},{5,4},{6,7},{7,6},{8,9},{9,8},{10,11... | collective-permute-start | bytes 786440 | tf_op jit(solution)/shard_map/ppermute | solution.py:296
  32.5 12.2 %collective-permute-start.9 = (bf16[64,2048]{1,0:T(8,128)(2,1)S(1)}, bf16[64,2048]{1,0:T(8,128)(2,1)S(1)}, u32[]{:S(2)}, u32[]{:S(2)}) collective-permute-start(bf16[64,2048]{1,0:T(8,128)(2,1)S(1)} %collective-permute-done.4.refs_3_), channel_id=1, source_target_pairs={{0,1},{1,0},{2,3},{3,2},{4,5},{5,4},{6,7},{7,6},{8,9},{9,8},{10,11... | collective-permute-start | bytes 786440 | tf_op jit(solution)/shard_map/ppermute | solution.py:296
  33.4 11.8 %collective-permute-start.5 = (bf16[64,2048]{1,0:T(8,128)(2,1)S(1)}, bf16[64,2048]{1,0:T(8,128)(2,1)S(1)}, u32[]{:S(2)}, u32[]{:S(2)}) collective-permute-start(bf16[64,2048]{1,0:T(8,128)(2,1)S(1)} %collective-permute-done.4.refs_3_), channel_id=1, source_target_pairs={{0,12},{4,0},{8,4},{12,8},{1,13},{5,1},{9,5},{13,9},{2,14},{6,2},{... | collective-permute-start | bytes 786440 | tf_op jit(solution)/shard_map/ppermute | solution.py:278
  36.1 11.4 %collective-permute-start.6 = (bf16[64,2048]{1,0:T(8,128)(2,1)S(1)}, bf16[64,2048]{1,0:T(8,128)(2,1)S(1)}, u32[]{:S(2)}, u32[]{:S(2)}) collective-permute-start(bf16[64,2048]{1,0:T(8,128)(2,1)S(1)} %collective-permute-done.3.refs_2_), channel_id=1, source_target_pairs={{0,2},{1,3},{4,6},{5,7},{8,10},{9,11},{12,14},{13,15},{16,18},{17,... | collective-permute-start | bytes 786440 | tf_op jit(solution)/shard_map/ppermute | solution.py:294
  39.3 8.1 %collective-permute-start.8 = (bf16[64,2048]{1,0:T(8,128)(2,1)S(1)}, bf16[64,2048]{1,0:T(8,128)(2,1)S(1)}, u32[]{:S(2)}, u32[]{:S(2)}) collective-permute-start(bf16[64,2048]{1,0:T(8,128)(2,1)S(1)} %collective-permute-done.3.refs_2_), channel_id=1, source_target_pairs={{0,1},{1,0},{2,3},{3,2},{4,5},{5,4},{6,7},{7,6},{8,9},{9,8},{10,11... | collective-permute-start | bytes 786440 | tf_op jit(solution)/shard_map/ppermute | solution.py:296
  44.7 2.8 %collective-permute-start.7 = (bf16[64,2048]{1,0:T(8,128)(2,1)S(1)}, bf16[64,2048]{1,0:T(8,128)(2,1)S(1)}, u32[]{:S(2)}, u32[]{:S(2)}) collective-permute-start(bf16[64,2048]{1,0:T(8,128)(2,1)S(1)} %collective-permute-done.2.refs_1_), channel_id=1, source_target_pairs={{0,1},{1,0},{2,3},{3,2},{4,5},{5,4},{6,7},{7,6},{8,9},{9,8},{10,11... | collective-permute-start | bytes 786440 | tf_op jit(solution)/shard_map/ppermute | solution.py:296
  44.7 2.8 %collective-permute-start.1 = (bf16[64,2048]{1,0:T(8,128)(2,1)S(1)}, bf16[64,2048]{1,0:T(8,128)(2,1)S(1)}, u32[]{:S(2)}, u32[]{:S(2)}) collective-permute-start(bf16[64,2048]{1,0:T(8,128)(2,1)S(1)} %collective-permute-done.refs_6_), channel_id=1, source_target_pairs={{0,1},{1,0},{2,3},{3,2},{4,5},{5,4},{6,7},{7,6},{8,9},{9,8},{10,11... | collective-permute-start | bytes 786440 | tf_op jit(solution)/shard_map/ppermute | solution.py:297
  45.2 3.4 %collective-permute-start.10 = (bf16[64,2048]{1,0:T(8,128)(2,1)S(1)}, bf16[64,2048]{1,0:T(8,128)(2,1)S(1)}, u32[]{:S(2)}, u32[]{:S(2)}) collective-permute-start(bf16[64,2048]{1,0:T(8,128)(2,1)S(1)} %collective-permute-done.5.refs_4_), channel_id=1, source_target_pairs={{0,1},{1,0},{2,3},{3,2},{4,5},{5,4},{6,7},{7,6},{8,9},{9,8},{10,11... | collective-permute-start | bytes 786440 | tf_op jit(solution)/shard_map/ppermute | solution.py:296
  47.5 1.5 %collective-permute-start.11 = (bf16[64,2048]{1,0:T(8,128)(2,1)S(1)}, bf16[64,2048]{1,0:T(8,128)(2,1)S(1)}, u32[]{:S(2)}, u32[]{:S(2)}) collective-permute-start(bf16[64,2048]{1,0:T(8,128)(2,1)S(1)} %collective-permute-done.6.refs_5_), channel_id=1, source_target_pairs={{0,1},{1,0},{2,3},{3,2},{4,5},{5,4},{6,7},{7,6},{8,9},{9,8},{10,11... | collective-permute-start | bytes 786440 | tf_op jit(solution)/shard_map/ppermute | solution.py:296

commit v6 on v5

--- a/solution.py
+++ b/solution.py
@@ -295,6 +295,7 @@
     ]
     swapped = [lax.ppermute(value, "core", [(0, 1), (1, 0)]) for value in held]
     held[0] = lax.ppermute(swapped[0], "core", [(0, 1), (1, 0)])
+    swapped[2] = lax.ppermute(second, "core", [(0, 1)])
     column = lax.axis_index("column")
     return correlate(core[None], column[None], held, swapped)
 

time: 65.2 us -> 65.2 us (level)
    ppermute x0 -> x1, starting transfers between devices: none -> 1.28 us  [body(): swapped[2] = lax.ppermute(second, 'core', [(0, 1)])]
    ppermute x6 -> x5, starting transfers between devices: 11.9 us -> 11 us  [body(): swapped = [lax.ppermute(value, 'core', [(0, 1), (1, 0)]) for value in held]]
    ppermute x6 -> x5, waiting for transfers between devices: 1.52 us -> 1.31 us  [body(): swapped = [lax.ppermute(value, 'core', [(0, 1), (1, 0)]) for value in held]]
  transfers between devices with their start and end apart: 12 -> 12, of which waited for: 3 -> 4; matrix products, arithmetic and copies ran while one was open for 0% -> 0% of each run, Pallas kernels for 0% -> 0%
where the time goes in v6:
time: 65.2 us; the launch traced here: 64 us
  Pallas kernels  23.9 us (37%)
  starting transfers between devices  21.2 us (33%)
  blocking collectives  15.3 us (23%)
  waiting for transfers between devices  3.48 us (5%)
    all_to_all x1, blocking collectives, body(): lax.all_to_all(parts, 'sub', split_axis=0, concat_axis=0, tiled=True)  15.3 us
    pallas_call x1, Pallas kernels, correlate(): pl.pallas_call(correlate_kernel, grid_spec=pltpu.PrefetchScalarGridSpec(n...  15 us
    ppermute x5, starting transfers between devices, body(): swapped = [lax.ppermute(value, 'core', [(0, 1), (1, 0)]) for value in held]  11 us
    pallas_call x1, Pallas kernels, filter_bank(): pl.pallas_call(filter_kernel, in_specs=[pl.BlockSpec(memory_space=pl.ANY)...  7.19 us
    ppermute x3, starting transfers between devices, up(): return lax.ppermute(value, 'row', pairs)  6.45 us
    ppermute x3, waiting for transfers between devices, up(): return lax.ppermute(value, 'row', pairs)  1.95 us
    pallas_call x1, Pallas kernels, assemble(): pl.pallas_call(assemble_kernel, out_shape=jax.ShapeDtypeStruct((2 * BLOCK...  1.74 us
    ppermute x5, waiting for transfers between devices, body(): swapped = [lax.ppermute(value, 'core', [(0, 1), (1, 0)]) for value in held]  1.31 us
  transfers between devices with their start and end apart: 12, of which 4 were waited for; matrix products, arithmetic and copies ran while one was open for 0% of the time, Pallas kernels for 0%

profile of v6, /device:TPU:3, one launch (start us, length us, event | category | flops | bytes accessed | tf_op | source)
XLA Modules:
  0.0 64.0 jit_solution(12208331474978722923)
XLA Ops:
  0.0 7.2 %filter_bank.1 = bf16[16,32,384]{2,1,0:T(8,128)(2,1)} custom-call(bf16[32,65536]{1,0:T(8,128)(2,1)} %x_hbm.1, s32[1,4096]{1,0:T(1,128)} %bitcast.3, f32[16,256]{1,0:T(8,128)} %constant.10.cos_hbm), custom_call_target="tpu_custom_call" | custom-call | tf_op jit(solution)/shard_map/filter_bank/pallas_call | solution.py:124
  7.2 15.3 %all_to_all.5.parts_ref = bf16[16,32,384]{2,1,0:T(8,128)(2,1)} all-to-all(bf16[16,32,384]{2,1,0:T(8,128)(2,1)} %filter_bank.1), channel_id=1, replica_groups=mesh['sub'=8,'row'=4,'column'=2,'core'=2] {'sub'}, dimensions={0} | all-to-all | bytes 786432 | tf_op jit(solution)/shard_map/all_to_all | solution.py:284
  22.5 1.7 %assemble.1 = bf16[64,2048]{1,0:T(8,128)(2,1)} custom-call(bf16[16,32,384]{2,1,0:T(8,128)(2,1)} %all_to_all.5.parts_ref), custom_call_target="tpu_custom_call" | custom-call | tf_op jit(solution)/shard_map/assemble/pallas_call | solution.py:158
  24.3 1.1 %collective-permute-start.4 = (bf16[64,2048]{1,0:T(8,128)(2,1)}, bf16[64,2048]{1,0:T(8,128)(2,1)S(1)}, u32[]{:S(2)}, u32[]{:S(2)}) collective-permute-start(bf16[64,2048]{1,0:T(8,128)(2,1)} %assemble.1), channel_id=1, source_target_pairs={{0,2},{2,0},{1,3},{3,1},{4,6},{6,4},{5,7},{7,5},{8,10},{10,8},{9,1... | collective-permute-start | bytes 786440 | tf_op jit(solution)/shard_map/ppermute | solution.py:287
  25.4 2.9 %collective-permute-start.3 = (bf16[64,2048]{1,0:T(8,128)(2,1)}, bf16[64,2048]{1,0:T(8,128)(2,1)S(1)}, u32[]{:S(2)}, u32[]{:S(2)}) collective-permute-start(bf16[64,2048]{1,0:T(8,128)(2,1)} %assemble.1), channel_id=1, source_target_pairs={{0,8},{4,12},{8,0},{12,4},{1,9},{5,13},{9,1},{13,5},{2,10},{6,14},... | collective-permute-start | bytes 786440 | tf_op jit(solution)/shard_map/ppermute | solution.py:278
  28.3 0.8 %collective-permute-start.2 = (bf16[64,2048]{1,0:T(8,128)(2,1)}, bf16[64,2048]{1,0:T(8,128)(2,1)S(1)}, u32[]{:S(2)}, u32[]{:S(2)}) collective-permute-start(bf16[64,2048]{1,0:T(8,128)(2,1)} %assemble.1), channel_id=1, source_target_pairs={{0,12},{4,0},{8,4},{12,8},{1,13},{5,1},{9,5},{13,9},{2,14},{6,2},{... | collective-permute-start | bytes 786440 | tf_op jit(solution)/shard_map/ppermute | solution.py:278
  29.1 3.4 %collective-permute-start = (bf16[64,2048]{1,0:T(8,128)(2,1)}, bf16[64,2048]{1,0:T(8,128)(2,1)S(1)}, u32[]{:S(2)}, u32[]{:S(2)}) collective-permute-start(bf16[64,2048]{1,0:T(8,128)(2,1)} %assemble.1), channel_id=1, source_target_pairs={{0,1},{1,0},{2,3},{3,2},{4,5},{5,4},{6,7},{7,6},{8,9},{9,8},{10,11... | collective-permute-start | bytes 786440 | tf_op jit(solution)/shard_map/ppermute | solution.py:296
  32.5 0.0 collective-permute-done.4.refs_3_
  32.5 0.9 %collective-permute-start.9 = (bf16[64,2048]{1,0:T(8,128)(2,1)S(1)}, bf16[64,2048]{1,0:T(8,128)(2,1)S(1)}, u32[]{:S(2)}, u32[]{:S(2)}) collective-permute-start(bf16[64,2048]{1,0:T(8,128)(2,1)S(1)} %collective-permute-done.4.refs_3_), channel_id=1, source_target_pairs={{0,1},{1,0},{2,3},{3,2},{4,5},{5,4},{6,7},{7,6},{8,9},{9,8},{10,11... | collective-permute-start | bytes 786440 | tf_op jit(solution)/shard_map/ppermute | solution.py:296
  33.4 2.7 %collective-permute-start.5 = (bf16[64,2048]{1,0:T(8,128)(2,1)S(1)}, bf16[64,2048]{1,0:T(8,128)(2,1)S(1)}, u32[]{:S(2)}, u32[]{:S(2)}) collective-permute-start(bf16[64,2048]{1,0:T(8,128)(2,1)S(1)} %collective-permute-done.4.refs_3_), channel_id=1, source_target_pairs={{0,12},{4,0},{8,4},{12,8},{1,13},{5,1},{9,5},{13,9},{2,14},{6,2},{... | collective-permute-start | bytes 786440 | tf_op jit(solution)/shard_map/ppermute | solution.py:278
  36.1 0.0 collective-permute-done.3.refs_2_
  36.1 1.3 %collective-permute-start.6 = (bf16[64,2048]{1,0:T(8,128)(2,1)S(1)}, bf16[64,2048]{1,0:T(8,128)(2,1)S(1)}, u32[]{:S(2)}, u32[]{:S(2)}) collective-permute-start(bf16[64,2048]{1,0:T(8,128)(2,1)S(1)} %collective-permute-done.3.refs_2_), channel_id=1, source_target_pairs={{0,2},{1,3},{4,6},{5,7},{8,10},{9,11},{12,14},{13,15},{16,18},{17,... | collective-permute-start | bytes 786440 | tf_op jit(solution)/shard_map/ppermute | solution.py:294
  37.4 1.9 %collective-permute-done.2.refs_1_ = bf16[64,2048]{1,0:T(8,128)(2,1)S(1)} collective-permute-done((bf16[64,2048]{1,0:T(8,128)(2,1)}, bf16[64,2048]{1,0:T(8,128)(2,1)S(1)}, u32[]{:S(2)}, u32[]{:S(2)}) %collective-permute-start.2) | collective-permute-done | bytes 262176 | tf_op jit(solution)/shard_map/ppermute | solution.py:278
  39.3 1.3 %collective-permute-start.8 = (bf16[64,2048]{1,0:T(8,128)(2,1)S(1)}, bf16[64,2048]{1,0:T(8,128)(2,1)S(1)}, u32[]{:S(2)}, u32[]{:S(2)}) collective-permute-start(bf16[64,2048]{1,0:T(8,128)(2,1)S(1)} %collective-permute-done.3.refs_2_), channel_id=1, source_target_pairs={{0,1},{2,3},{4,5},{6,7},{8,9},{10,11},{12,13},{14,15},{16,17},{18,... | collective-permute-start | bytes 786440 | tf_op jit(solution)/shard_map/ppermute | solution.py:298
  40.6 0.0 collective-permute-done.refs_6_
  40.6 5.4 %collective-permute-start.7 = (bf16[64,2048]{1,0:T(8,128)(2,1)S(1)}, bf16[64,2048]{1,0:T(8,128)(2,1)S(1)}, u32[]{:S(2)}, u32[]{:S(2)}) collective-permute-start(bf16[64,2048]{1,0:T(8,128)(2,1)S(1)} %collective-permute-done.2.refs_1_), channel_id=1, source_target_pairs={{0,1},{1,0},{2,3},{3,2},{4,5},{5,4},{6,7},{7,6},{8,9},{9,8},{10,11... | collective-permute-start | bytes 786440 | tf_op jit(solution)/shard_map/ppermute | solution.py:296
  46.1 0.0 collective-permute-done.9.refs_9_
  46.1 0.1 collective-permute-start.1
  46.2 0.0 collective-permute-done.5.refs_4_
  46.2 1.3 %collective-permute-start.10 = (bf16[64,2048]{1,0:T(8,128)(2,1)S(1)}, bf16[64,2048]{1,0:T(8,128)(2,1)S(1)}, u32[]{:S(2)}, u32[]{:S(2)}) collective-permute-start(bf16[64,2048]{1,0:T(8,128)(2,1)S(1)} %collective-permute-done.5.refs_4_), channel_id=1, source_target_pairs={{0,1},{1,0},{2,3},{3,2},{4,5},{5,4},{6,7},{7,6},{8,9},{9,8},{10,11... | collective-permute-start | bytes 786440 | tf_op jit(solution)/shard_map/ppermute | solution.py:296
  47.5 0.0 collective-permute-done.6.refs_5_
  47.5 0.0 collective-permute-start.11
  47.5 0.0 collective-permute-done.8.refs_8_
  47.5 0.0 collective-permute-done.7.refs_7_
  47.5 0.2 collective-permute-done.1.refs_0_
  47.7 0.9 %collective-permute-done.10.refs_10_ = bf16[64,2048]{1,0:T(8,128)(2,1)S(1)} collective-permute-done((bf16[64,2048]{1,0:T(8,128)(2,1)S(1)}, bf16[64,2048]{1,0:T(8,128)(2,1)S(1)}, u32[]{:S(2)}, u32[]{:S(2)}) %collective-permute-start.10) | collective-permute-done | bytes 262176 | tf_op jit(solution)/shard_map/ppermute | solution.py:296
  48.6 0.4 collective-permute-done.11.refs_11_
  49.0 15.0 %correlate.1 = bf16[2,32,288,128]{3,2,1,0:T(8,128)(2,1)} custom-call(s32[1]{0:T(128)} %bitcast.core_ref, s32[1]{0:T(128)} %bitcast.1.column_ref, bf16[64,2048]{1,0:T(8,128)(2,1)S(1)} %collective-permute-done.1.refs_0_, bf16[64,2048]{1,0:T(8,128)(2,1)S(1)} %collective-permute-done.2.refs_1_, bf16[64,2048]{1,0:T(8,128)(2,1)S(1)} %collective-permute-done.3.refs_2_, ...), custom_call_target="tpu_custom_call" | custom-call | flops 9663676416 | bytes 8388608 | tf_op jit(solution)/shard_map/correlate/pallas_call | solution.py:252
Async XLA Ops:
  24.3 8.2 %collective-permute-start.4 = (bf16[64,2048]{1,0:T(8,128)(2,1)}, bf16[64,2048]{1,0:T(8,128)(2,1)S(1)}, u32[]{:S(2)}, u32[]{:S(2)}) collective-permute-start(bf16[64,2048]{1,0:T(8,128)(2,1)} %assemble.1), channel_id=1, source_target_pairs={{0,2},{2,0},{1,3},{3,1},{4,6},{6,4},{5,7},{7,5},{8,10},{10,8},{9,1... | collective-permute-start | bytes 786440 | tf_op jit(solution)/shard_map/ppermute | solution.py:287
  25.4 10.7 %collective-permute-start.3 = (bf16[64,2048]{1,0:T(8,128)(2,1)}, bf16[64,2048]{1,0:T(8,128)(2,1)S(1)}, u32[]{:S(2)}, u32[]{:S(2)}) collective-permute-start(bf16[64,2048]{1,0:T(8,128)(2,1)} %assemble.1), channel_id=1, source_target_pairs={{0,8},{4,12},{8,0},{12,4},{1,9},{5,13},{9,1},{13,5},{2,10},{6,14},... | collective-permute-start | bytes 786440 | tf_op jit(solution)/shard_map/ppermute | solution.py:278
  28.3 11.0 %collective-permute-start.2 = (bf16[64,2048]{1,0:T(8,128)(2,1)}, bf16[64,2048]{1,0:T(8,128)(2,1)S(1)}, u32[]{:S(2)}, u32[]{:S(2)}) collective-permute-start(bf16[64,2048]{1,0:T(8,128)(2,1)} %assemble.1), channel_id=1, source_target_pairs={{0,12},{4,0},{8,4},{12,8},{1,13},{5,1},{9,5},{13,9},{2,14},{6,2},{... | collective-permute-start | bytes 786440 | tf_op jit(solution)/shard_map/ppermute | solution.py:278
  29.1 11.5 %collective-permute-start = (bf16[64,2048]{1,0:T(8,128)(2,1)}, bf16[64,2048]{1,0:T(8,128)(2,1)S(1)}, u32[]{:S(2)}, u32[]{:S(2)}) collective-permute-start(bf16[64,2048]{1,0:T(8,128)(2,1)} %assemble.1), channel_id=1, source_target_pairs={{0,1},{1,0},{2,3},{3,2},{4,5},{5,4},{6,7},{7,6},{8,9},{9,8},{10,11... | collective-permute-start | bytes 786440 | tf_op jit(solution)/shard_map/ppermute | solution.py:296
  32.5 13.6 %collective-permute-start.9 = (bf16[64,2048]{1,0:T(8,128)(2,1)S(1)}, bf16[64,2048]{1,0:T(8,128)(2,1)S(1)}, u32[]{:S(2)}, u32[]{:S(2)}) collective-permute-start(bf16[64,2048]{1,0:T(8,128)(2,1)S(1)} %collective-permute-done.4.refs_3_), channel_id=1, source_target_pairs={{0,1},{1,0},{2,3},{3,2},{4,5},{5,4},{6,7},{7,6},{8,9},{9,8},{10,11... | collective-permute-start | bytes 786440 | tf_op jit(solution)/shard_map/ppermute | solution.py:296
  33.4 12.8 %collective-permute-start.5 = (bf16[64,2048]{1,0:T(8,128)(2,1)S(1)}, bf16[64,2048]{1,0:T(8,128)(2,1)S(1)}, u32[]{:S(2)}, u32[]{:S(2)}) collective-permute-start(bf16[64,2048]{1,0:T(8,128)(2,1)S(1)} %collective-permute-done.4.refs_3_), channel_id=1, source_target_pairs={{0,12},{4,0},{8,4},{12,8},{1,13},{5,1},{9,5},{13,9},{2,14},{6,2},{... | collective-permute-start | bytes 786440 | tf_op jit(solution)/shard_map/ppermute | solution.py:278
  36.1 11.4 %collective-permute-start.6 = (bf16[64,2048]{1,0:T(8,128)(2,1)S(1)}, bf16[64,2048]{1,0:T(8,128)(2,1)S(1)}, u32[]{:S(2)}, u32[]{:S(2)}) collective-permute-start(bf16[64,2048]{1,0:T(8,128)(2,1)S(1)} %collective-permute-done.3.refs_2_), channel_id=1, source_target_pairs={{0,2},{1,3},{4,6},{5,7},{8,10},{9,11},{12,14},{13,15},{16,18},{17,... | collective-permute-start | bytes 786440 | tf_op jit(solution)/shard_map/ppermute | solution.py:294
  39.3 8.1 %collective-permute-start.8 = (bf16[64,2048]{1,0:T(8,128)(2,1)S(1)}, bf16[64,2048]{1,0:T(8,128)(2,1)S(1)}, u32[]{:S(2)}, u32[]{:S(2)}) collective-permute-start(bf16[64,2048]{1,0:T(8,128)(2,1)S(1)} %collective-permute-done.3.refs_2_), channel_id=1, source_target_pairs={{0,1},{2,3},{4,5},{6,7},{8,9},{10,11},{12,13},{14,15},{16,17},{18,... | collective-permute-start | bytes 786440 | tf_op jit(solution)/shard_map/ppermute | solution.py:298
  40.6 6.8 %collective-permute-start.7 = (bf16[64,2048]{1,0:T(8,128)(2,1)S(1)}, bf16[64,2048]{1,0:T(8,128)(2,1)S(1)}, u32[]{:S(2)}, u32[]{:S(2)}) collective-permute-start(bf16[64,2048]{1,0:T(8,128)(2,1)S(1)} %collective-permute-done.2.refs_1_), channel_id=1, source_target_pairs={{0,1},{1,0},{2,3},{3,2},{4,5},{5,4},{6,7},{7,6},{8,9},{9,8},{10,11... | collective-permute-start | bytes 786440 | tf_op jit(solution)/shard_map/ppermute | solution.py:296
  46.1 1.6 %collective-permute-start.1 = (bf16[64,2048]{1,0:T(8,128)(2,1)S(1)}, bf16[64,2048]{1,0:T(8,128)(2,1)S(1)}, u32[]{:S(2)}, u32[]{:S(2)}) collective-permute-start(bf16[64,2048]{1,0:T(8,128)(2,1)S(1)} %collective-permute-done.refs_6_), channel_id=1, source_target_pairs={{0,1},{1,0},{2,3},{3,2},{4,5},{5,4},{6,7},{7,6},{8,9},{9,8},{10,11... | collective-permute-start | bytes 786440 | tf_op jit(solution)/shard_map/ppermute | solution.py:297
  46.2 2.5 %collective-permute-start.10 = (bf16[64,2048]{1,0:T(8,128)(2,1)S(1)}, bf16[64,2048]{1,0:T(8,128)(2,1)S(1)}, u32[]{:S(2)}, u32[]{:S(2)}) collective-permute-start(bf16[64,2048]{1,0:T(8,128)(2,1)S(1)} %collective-permute-done.5.refs_4_), channel_id=1, source_target_pairs={{0,1},{1,0},{2,3},{3,2},{4,5},{5,4},{6,7},{7,6},{8,9},{9,8},{10,11... | collective-permute-start | bytes 786440 | tf_op jit(solution)/shard_map/ppermute | solution.py:296
  47.5 1.5 %collective-permute-start.11 = (bf16[64,2048]{1,0:T(8,128)(2,1)S(1)}, bf16[64,2048]{1,0:T(8,128)(2,1)S(1)}, u32[]{:S(2)}, u32[]{:S(2)}) collective-permute-start(bf16[64,2048]{1,0:T(8,128)(2,1)S(1)} %collective-permute-done.6.refs_5_), channel_id=1, source_target_pairs={{0,1},{1,0},{2,3},{3,2},{4,5},{5,4},{6,7},{7,6},{8,9},{9,8},{10,11... | collective-permute-start | bytes 786440 | tf_op jit(solution)/shard_map/ppermute | solution.py:296
